TPU v7x, 256 devices: a whole 4x4x8 slice. The times are simulated.
256 devices in a mesh: dp: 4 (over y), seq: 64 (over x, z, core).
Axes of the slice: x: 4, y: 4, z: 8, core: 2. Of those that a mesh axis runs over, the one named last changes fastest.
Arguments:
- grid_fields: bfloat16 [4, 100, 262144], P('dp', None, 'seq'), may hold values from -6 to 6
- mesh_latent: bfloat16 [16384, 1024], P('seq'), may hold values from -6 to 6
- edge_source: int32 [64, 64, 128], P('seq'), may hold values from 0 to 4095
- edge_target: int32 [64, 64, 128], P('seq'), may hold values from 0 to 255, as said below
- edge_count: int32 [64, 64], replicated, may hold values from 0 to 128, as said below
- edge_bias: float32 [64, 64, 128], P('seq'), may hold values from -6 to 300
- encoder_proj: bfloat16 [100, 2048], replicated, may hold values from -0.625 to 0.625
- norm_gain: float32 [1024], replicated, may hold values from 0.5 to 1.5
- processor_proj: bfloat16 [1024, 3072], replicated, may hold values from -0.1875 to 0.1875
- offset_bias: float32 [16, 257], replicated, may hold values from -6 to 300
- windows: int32 [16], replicated, may hold values from 4 to 128, as said below
- output_proj: bfloat16 [1024, 1024], replicated, may hold values from -0.1875 to 0.1875
- cotangent: bfloat16 [4, 16384, 1024], P('dp', 'seq'), may hold values from -6 to 6
Outputs:
- processed: bfloat16 [4, 16384, 1024], P('dp', 'seq')
- output_grad: float32 [1024, 1024], P('seq')
Inputs may be any that keep to these rules, and one draw needn't show every extreme that they name: `edge_target`: slots 2m and 2m + 1 of a block name the same row. `edge_count`: in every draw one owner receives 128 live slots from every source device. `windows`: some head's reach is exactly 128.
All inputs are finite; a program needn't handle non-finite values.
Results may differ from a plain program's by a relative error of at most 0.02.
Values may be sent and summed in bfloat16 or wider, within the bound.
A program may use at most 192 MiB of HBM per device.

v0:
```python
import math

import jax
import jax.numpy as jnp
from jax import lax
from jax.sharding import PartitionSpec as P


def with_halo(shard, sides, width):
    for axis, dim in sides:
        size, length = (lax.axis_size(axis), shard.shape[dim])
        up = [(i, (i + 1) % size) for i in range(size - 1)]
        down = [(j, i) for i, j in up]
        last = lax.slice_in_dim(shard, length - width, length, axis=dim)
        first = lax.slice_in_dim(shard, 0, width, axis=dim)
        before = lax.ppermute(last, axis, up)
        after = lax.ppermute(first, axis, down)
        shard = jnp.concatenate([before, shard, after], axis=dim)
    return shard


def attend_edges(running, slot_values, targets, slot_bias, is_live, latent, head_count):
    running_max, running_sum, running_acc = running
    node_count, model_width = latent.shape
    head_size = model_width // head_count
    slot_count = targets.shape[0]
    key_part = slot_values[:, :model_width].reshape(slot_count, head_count, head_size)
    value_part = slot_values[:, model_width:].reshape(slot_count, head_count, head_size)
    queries = (
        jnp.take(latent, targets, axis=0)
        .astype(jnp.float32)
        .reshape(slot_count, head_count, head_size)
    )
    scores = jnp.sum(queries * key_part, axis=-1) / math.sqrt(head_size) + slot_bias[:, None]
    scores = jnp.where(is_live[:, None], scores, -1e30)
    member = targets[:, None] == jnp.arange(node_count, dtype=jnp.int32)[None, :]

    def head_max(column):
        return jnp.max(jnp.where(member, column[:, None], -1e30), axis=0)

    block_max = lax.map(head_max, scores.T).T
    new_max = jnp.maximum(running_max, block_max)
    factor = jnp.exp(running_max - new_max)
    selector = member.astype(jnp.float32)
    slot_max = jnp.dot(selector, new_max, precision=lax.Precision.HIGHEST)
    weights = jnp.exp(scores - slot_max)
    contract = (((0,), (0,)), ((), ()))
    weight_sums = lax.dot_general(selector, weights, contract, precision=lax.Precision.HIGHEST)
    weighted = (weights[:, :, None] * value_part).reshape(slot_count, model_width)
    upper_part = weighted.astype(jnp.bfloat16)
    lower_part = (weighted - upper_part.astype(jnp.float32)).astype(jnp.bfloat16)
    selector_half = member.astype(jnp.bfloat16)
    value_sums = lax.dot_general(
        selector_half, upper_part, contract, preferred_element_type=jnp.float32
    )
    value_sums = value_sums + lax.dot_general(
        selector_half, lower_part, contract, preferred_element_type=jnp.float32
    )
    running_sum = running_sum * factor + weight_sums
    running_acc = running_acc * factor[:, :, None] + value_sums.reshape(
        node_count, head_count, head_size
    )
    return (new_max, running_sum, running_acc)


def layer_norm(state, gain):
    center = state - jnp.mean(state, axis=-1, keepdims=True)
    variance = jnp.mean(center * center, axis=-1, keepdims=True)
    return (center * lax.rsqrt(variance + 1e-05) * gain).astype(jnp.bfloat16)


def window_attention(queries, extended, offset_bias, windows, first_row, row_total, reach):
    query_count, model_width = queries.shape
    head_count = offset_bias.shape[0]
    head_size = model_width // head_count
    key_count = extended.shape[0]
    query_heads = queries.reshape(query_count, head_count, head_size)
    key_heads = extended[:, :model_width].reshape(key_count, head_count, head_size)
    value_heads = extended[:, model_width:].reshape(key_count, head_count, head_size)
    scores = jnp.einsum(
        "qhd,khd->hqk", query_heads, key_heads, preferred_element_type=jnp.float32
    ) / math.sqrt(head_size)
    offset = (
        jnp.arange(key_count, dtype=jnp.int32)[None, :]
        - reach
        - jnp.arange(query_count, dtype=jnp.int32)[:, None]
    )
    key_rows = first_row - reach + jnp.arange(key_count, dtype=jnp.int32)
    inside = (key_rows >= 0) & (key_rows < row_total)
    offset_table = jnp.take(offset_bias, jnp.clip(offset + reach, 0, 2 * reach), axis=1)
    allowed = inside[None, None, :] & (jnp.abs(offset)[None, :, :] <= windows[:, None, None])
    scores = jnp.where(allowed, scores + offset_table, -1e30)
    peak = jnp.max(scores, axis=-1, keepdims=True)
    powered = jnp.exp(scores - peak)
    weights = (powered / jnp.sum(powered, axis=-1, keepdims=True)).astype(jnp.bfloat16)
    mixture = jnp.einsum("hqk,khd->qhd", weights, value_heads, preferred_element_type=jnp.float32)
    return mixture.reshape(query_count, model_width).astype(jnp.bfloat16)


def shards(
    grid_fields,
    mesh_latent,
    edge_source,
    edge_target,
    edge_count,
    edge_bias,
    encoder_proj,
    norm_gain,
    processor_proj,
    offset_bias,
    windows,
    output_proj,
    cotangent,
):
    shard_count = lax.axis_size("seq")
    device = lax.axis_index("seq")
    node_count, model_width = mesh_latent.shape
    head_count = offset_bias.shape[0]
    head_size = model_width // head_count
    reach = (offset_bias.shape[1] - 1) // 2
    channels = grid_fields.shape[1]
    capacity = edge_source.shape[2]
    outgoing = jnp.take(grid_fields[0], edge_source[0].reshape(-1), axis=1).reshape(
        channels, shard_count, capacity
    )
    incoming = lax.all_to_all(outgoing, "seq", split_axis=1, concat_axis=1, tiled=True)
    own_counts = lax.dynamic_index_in_dim(edge_count, device, 1, keepdims=False)
    is_live = jnp.arange(capacity, dtype=jnp.int32)[None, :] < own_counts[:, None]
    group = max(1, min(shard_count, 2048 // capacity))
    while shard_count % group:
        group = group - 1
    block_count = shard_count // group
    block_slots = group * capacity
    feature_blocks = incoming.reshape(channels, block_count, block_slots).transpose(1, 0, 2)
    target_blocks = edge_target[0].reshape(block_count, block_slots)
    bias_blocks = edge_bias[0].reshape(block_count, block_slots)
    live_blocks = is_live.reshape(block_count, block_slots)

    def source_step(running, pieces):
        features, targets, slot_bias, live_flags = pieces
        slot_values = lax.dot_general(
            features, encoder_proj, (((0,), (0,)), ((), ())), preferred_element_type=jnp.float32
        )
        return (
            attend_edges(
                running, slot_values, targets, slot_bias, live_flags, mesh_latent, head_count
            ),
            None,
        )

    initial = (
        jnp.zeros((node_count, head_count), jnp.float32),
        jnp.ones((node_count, head_count), jnp.float32),
        jnp.zeros((node_count, head_count, head_size), jnp.float32),
    )
    running, unused = lax.scan(
        source_step, initial, (feature_blocks, target_blocks, bias_blocks, live_blocks)
    )
    encoded = (running[2] / running[1][:, :, None]).reshape(node_count, model_width)
    hidden_state = mesh_latent.astype(jnp.float32) + encoded
    normalized = layer_norm(hidden_state, norm_gain)
    projected_all = jnp.dot(normalized, processor_proj, preferred_element_type=jnp.float32).astype(
        jnp.bfloat16
    )
    queries = projected_all[:, :model_width]
    own_pairs = projected_all[:, model_width:]
    extended = with_halo(own_pairs, (("seq", 0),), reach)
    attended = window_attention(
        queries,
        extended,
        offset_bias,
        windows,
        device * node_count,
        node_count * shard_count,
        reach,
    )
    processed = (
        hidden_state + jnp.dot(attended, output_proj, preferred_element_type=jnp.float32)
    ).astype(jnp.bfloat16)
    local_grad = lax.dot_general(
        attended, cotangent[0], (((0,), (0,)), ((), ())), preferred_element_type=jnp.float32
    )
    share = model_width // shard_count
    summed = lax.psum(local_grad, ("dp", "seq"))
    gradient = lax.dynamic_slice_in_dim(summed, device * share, share, 0)
    return (processed[None], gradient)


def solution(mesh):
    in_specs = (
        P("dp", None, "seq"),
        P("seq", None),
        P("seq", None, None),
        P("seq", None, None),
        P(),
        P("seq", None, None),
        P(),
        P(),
        P(),
        P(),
        P(),
        P(),
        P("dp", "seq", None),
    )
    out_specs = (P("dp", "seq", None), P("seq", None))
    return jax.shard_map(shards, mesh=mesh, in_specs=in_specs, out_specs=out_specs, check_vma=False)
```

profile of v0, /device:TPU:32, one launch (start us, length us, event | category | flops | bytes accessed | tf_op | source)
XLA Modules:
  0.0 1124.9 jit_solution(9276478424915313065)
XLA Ops:
  11.2 29.4 %gather_fusion.1 = bf16[8192,100]{1,0:T(8,128)(2,1)} fusion(bf16[100,4096]{0,1:T(8,128)(2,1)} %bitcast.113, s32[8192]{0:T(1024)S(1)} %broadcast_clamp_fusion.2), kind=kCustom, calls=%fused_computation.1 | custom fusion | bytes 3309568 | tf_op jit(solution)/shard_map/jit(_take)/gather | solution.py:123
  47.5 11.8 %all-to-all-start = ((bf16[100,64,128]{2,0,1:T(8,128)(2,1)}), bf16[100,64,128]{2,0,1:T(8,128)(2,1)}, u32[]{:S(2)}, u32[]{:S(2)}) async-start(bf16[100,64,128]{2,0,1:T(8,128)(2,1)} %broadcast_select_fusion), calls=%async_computation | async-start | bytes 3407872 | tf_op jit(solution)/shard_map/all_to_all | solution.py:126
  62.0 430.4 %gather_fusion.2 = f32[131072,16]{1,0:T(8,128)} fusion(f32[16,257]{0,1:T(8,128)S(1)} %copy.57, s32[131072]{0:T(1024)S(1)} %broadcast_clamp_fusion.1), kind=kCustom, calls=%fused_computation.2 | custom fusion | bytes 17301504 | tf_op jit(solution)/shard_map/jit(_take)/gather | solution.py:90
  492.5 38.3 %copy.59 = f32[256,512,16]{1,0,2:T(8,128)} copy(f32[256,512,16]{2,1,0:T(8,128)} %bitcast.12) | data formatting | bytes 16777216 | tf_op jit(solution)/shard_map/jit(_take)/gather | solution.py:90
  541.7 243.1 %while.28 = (s32[]{:T(128)}, f32[256,16]{0,1:T(8,128)S(1)}, f32[256,16]{0,1:T(8,128)S(1)}, f32[256,16,64]{0,2,1:T(8,128)}, pred[4,2048]{1,0:T(4,128)(4,1)S(1)}, ...) while((s32[]{:T(128)}, f32[256,16]{0,1:T(8,128)S(1)}, ...), condition=%wide.region_5.6_spmd.clone, body=%wide.region_0.5_spmd.clone.sunk | while | flops 3212553984 | bytes 81764120 | solution.py:156
  541.7 9.1 fusion.86
  550.8 9.7 gather_fusion
  560.5 6.5 copy.65
  567.0 6.2 multiply_reduce_fusion.3
  573.4 12.8 %while.29 = (s32[]{:T(128)}, f32[16,256]{1,0:T(8,128)S(1)}, f32[16,2048]{1,0:T(8,128)S(1)}, s32[2048]{0:T(1024)S(1)}, s32[]{:T(128)}, /*index=5*/s32[]{:T(128)}) while((s32[]{:T(128)}, f32[16,256]{1,0:T(8,128)S(1)}, f32[16,2048]{1,0:T(8,128)S(1)}, s32[2048]{0:T(1024)S(1)}, s32[]{:T(128)}, /*index=5*/s32[]{:T(128)}) %tuple.70), condition=%wide.region_4.4_spmd.clone, body=%wide.region_2.3_spmd.clone.sunk | while | flops 1572610 | bytes 35917 | solution.py:41
  587.5 4.4 subtract_convert_fusion.2
  602.2 9.1 fusion.86
  611.3 9.7 gather_fusion
  621.0 6.5 copy.65
  627.5 6.2 multiply_reduce_fusion.3
  633.9 12.8 %while.29 = (s32[]{:T(128)}, f32[16,256]{1,0:T(8,128)S(1)}, f32[16,2048]{1,0:T(8,128)S(1)}, s32[2048]{0:T(1024)S(1)}, s32[]{:T(128)}, /*index=5*/s32[]{:T(128)}) while((s32[]{:T(128)}, f32[16,256]{1,0:T(8,128)S(1)}, f32[16,2048]{1,0:T(8,128)S(1)}, s32[2048]{0:T(1024)S(1)}, s32[]{:T(128)}, /*index=5*/s32[]{:T(128)}) %tuple.70), condition=%wide.region_4.4_spmd.clone, body=%wide.region_2.3_spmd.clone.sunk | while | flops 1572610 | bytes 35917 | solution.py:41
  648.0 4.4 subtract_convert_fusion.2
  663.0 9.1 fusion.86
  672.2 9.7 gather_fusion
  681.8 6.5 copy.65
  688.3 6.2 multiply_reduce_fusion.3
  694.7 12.8 %while.29 = (s32[]{:T(128)}, f32[16,256]{1,0:T(8,128)S(1)}, f32[16,2048]{1,0:T(8,128)S(1)}, s32[2048]{0:T(1024)S(1)}, s32[]{:T(128)}, /*index=5*/s32[]{:T(128)}) while((s32[]{:T(128)}, f32[16,256]{1,0:T(8,128)S(1)}, f32[16,2048]{1,0:T(8,128)S(1)}, s32[2048]{0:T(1024)S(1)}, s32[]{:T(128)}, /*index=5*/s32[]{:T(128)}) %tuple.70), condition=%wide.region_4.4_spmd.clone, body=%wide.region_2.3_spmd.clone.sunk | while | flops 1572610 | bytes 35917 | solution.py:41
  723.9 9.1 fusion.86
  733.0 9.7 gather_fusion
  742.6 6.5 copy.65
  749.2 6.2 multiply_reduce_fusion.3
  755.5 12.8 %while.29 = (s32[]{:T(128)}, f32[16,256]{1,0:T(8,128)S(1)}, f32[16,2048]{1,0:T(8,128)S(1)}, s32[2048]{0:T(1024)S(1)}, s32[]{:T(128)}, /*index=5*/s32[]{:T(128)}) while((s32[]{:T(128)}, f32[16,256]{1,0:T(8,128)S(1)}, f32[16,2048]{1,0:T(8,128)S(1)}, s32[2048]{0:T(1024)S(1)}, s32[]{:T(128)}, /*index=5*/s32[]{:T(128)}) %tuple.70), condition=%wide.region_4.4_spmd.clone, body=%wide.region_2.3_spmd.clone.sunk | while | flops 1572610 | bytes 35917 | solution.py:41
  769.6 4.4 subtract_convert_fusion.2
  792.7 5.0 convolution_convert_fusion
  816.9 7.1 fusion.25
  829.8 13.4 %fusion.27 = bf16[16,64,256]{2,1,0:T(8,128)(2,1)S(1)} fusion(bf16[512,16,64]{0,2,1:T(8,128)(2,1)} %bitcast.127, f32[16,256]{1,0:T(8,128)S(1)} %fusion.48, f32[16,256,512]{2,1,0:T(8,128)} %copy-done.2), kind=kOutput, calls=%fused_computation.54 | convolution fusion | flops 274993664 | bytes 9977856 | tf_op jit(solution)/shard_map/hqk,khd->qhd/dot_general | solution.py:96
  849.8 266.8 %all-reduce.2.cloned.1.call-done = f32[1024,1024]{1,0:T(8,128)} async-done(((f32[1024,1024]{1,0:T(8,128)}), f32[1024,1024]{1,0:T(8,128)}) %all-reduce.2.cloned.1.call-update) | async-done | bytes 4194320 | tf_op jit(solution)/shard_map/psum | solution.py:184
  (325 shorter events, 166.5 us)
Async XLA Ops:
  7.2 839.9 %copy-start = (bf16[1024,1024]{1,0:T(8,128)(2,1)S(1)}, bf16[1024,1024]{1,0:T(8,128)(2,1)}, u32[]{:S(2)}) copy-start(bf16[1024,1024]{1,0:T(8,128)(2,1)} %param.28) | copy-start | bytes 6291460
  44.6 14.7 %copy-start.6 = (s32[64,64]{1,0:T(8,128)S(1)}, s32[64,64]{1,0:T(8,128)}, u32[]{:S(2)}) copy-start(s32[64,64]{1,0:T(8,128)} %param.21) | copy-start | bytes 49156
  44.6 15.0 %copy-start.7 = (s32[1,64,128]{2,1,0:T(8,128)S(1)}, s32[1,64,128]{2,1,0:T(8,128)}, u32[]{:S(2)}) copy-start(s32[1,64,128]{2,1,0:T(8,128)} %param.20) | copy-start | bytes 98308
  44.6 15.0 %copy-start.8 = (f32[1,64,128]{2,1,0:T(8,128)S(1)}, f32[1,64,128]{2,1,0:T(8,128)}, u32[]{:S(2)}) copy-start(f32[1,64,128]{2,1,0:T(8,128)} %param.22) | copy-start | bytes 98308
  44.6 16.2 %copy-start.9 = (f32[16,257]{1,0:T(8,128)S(1)}, f32[16,257]{1,0:T(8,128)}, u32[]{:S(2)}) copy-start(f32[16,257]{1,0:T(8,128)} %param.26) | copy-start | bytes 49348
  47.5 483.4 %all-to-all-start = ((bf16[100,64,128]{2,0,1:T(8,128)(2,1)}), bf16[100,64,128]{2,0,1:T(8,128)(2,1)}, u32[]{:S(2)}, u32[]{:S(2)}) async-start(bf16[100,64,128]{2,0,1:T(8,128)(2,1)} %broadcast_select_fusion), calls=%async_computation | async-start | bytes 3407872 | tf_op jit(solution)/shard_map/all_to_all | solution.py:126
  59.3 1057.3 %all-reduce.2.cloned.1.call-start = ((), (), s32[]{:S(2)}) async-start(), calls=%async_computation.1 | async-start | bytes 8388608 | tf_op jit(solution)/shard_map/psum | solution.py:184
  59.4 433.1 %copy-start.4 = (s32[512]{0:T(512)}, s32[512]{0:T(512)S(1)}, u32[]{:S(2)}) copy-start(s32[512]{0:T(512)S(1)} %iota_add_fusion) | copy-start | bytes 6148
  530.9 10.8 copy-start.1
  530.9 10.8 copy-start.3
  784.8 8.0 copy-start.11
  792.7 11.7 %copy-start.5 = (s32[512]{0:T(512)S(1)}, s32[512]{0:T(512)}, u32[]{:S(2)}) copy-start(s32[512]{0:T(512)} %copy-done.4) | copy-start | bytes 6148
  798.8 10.8 collective-permute-start
  800.9 10.5 collective-permute-start.1
  813.1 3.8 copy-start.10
  824.0 3.5 copy-start.2
Sparse Core Ops, SparseCore 0:
  847.1 269.3 all-reduce.1
where the time goes:
time: 1130 us; the launch traced here: 1120 us
  local copies, waits for them, and re-layouts  611 us (54%)
  waiting for transfers between devices  269 us (24%)
  other arithmetic  116 us (10%)
  matrix products  94.5 us (8%)
  starting transfers between devices  17.4 us (2%)
  between operations  14.3 us (1%)
    gather x2, local copies, waits for them, and re-layouts, window_attention(): jnp.take(offset_bias, jnp.clip(offset + reach, 0, 2 * reach), axis=1)  469 us
    psum x1, waiting for transfers between devices, shards(): summed = lax.psum(local_grad, ('dp', 'seq'))  267 us
    gather x8, local copies, waits for them, and re-layouts, attend_edges(): jnp.take(latent, targets, axis=0).astype(jnp.float32)  64.7 us
    reduce_max x64, other arithmetic, head_max(): return jnp.max(jnp.where(member, column[:, None], -1e+30), axis=0)  45.5 us
    dot_general x4, matrix products, source_step(): lax.dot_general(features, encoder_proj, (((0,), (0,)), ((), ())), preferr...  36.4 us
    gather x2, local copies, waits for them, and re-layouts, shards(): jnp.take(grid_fields[0], edge_source[0].reshape(-1), axis=1)  33.4 us
    reduce_sum x4, other arithmetic, attend_edges(): jnp.sum(queries * key_part, axis=-1) / math.sqrt(head_size)  24.9 us
  transfers between devices with their start and end apart: 4, of which 3 were waited for; matrix products, arithmetic and copies ran while one was open for 43% of the time, Pallas kernels for 0%

commit v1 on v0

v1 whole, which is shorter than its diff:
```python
import functools

import jax
import jax.numpy as jnp
from jax import lax
from jax.experimental import pallas as pl
from jax.experimental.pallas import tpu as pltpu
from jax.sharding import PartitionSpec as P

MESH = pl.DeviceIdType.MESH
X, Z, CORES, Y = 4, 8, 2, 4
NEG = -1e30
F32 = jnp.float32
BF16 = jnp.bfloat16
VMEM_LIMIT = 56 * 1024 * 1024

NT = (((1,), (1,)), ((), ()))
TN = (((0,), (0,)), ((), ()))


def vmem():
    return pl.BlockSpec(memory_space=pltpu.VMEM)


def gather_kernel(source_ref, grid_ref, out_ref, table, stage):
    channels = grid_ref.shape[1]
    owners, capacity = source_ref.shape
    stage[...] = jnp.zeros_like(stage)

    def turn(chunk, carry):
        start = pl.multiple_of(chunk * 128, 128)
        stage[0:channels, :] = grid_ref[0, :, pl.ds(start, 128)].astype(F32)
        table[pl.ds(start, 128), :] = stage[...].T
        return carry

    lax.fori_loop(0, grid_ref.shape[2] // 128, turn, 0)

    def owner_step(owner, carry):
        for slot in range(capacity):
            row = (slot % 2) * (capacity // 2) + slot // 2
            stage[row : row + 1, :] = table[pl.ds(source_ref[owner, slot], 1), :]
        out_ref[owner] = stage[...].astype(BF16)
        return carry

    lax.fori_loop(0, owners, owner_step, 0)


def edge_kernel(
    field_ref, target_ref, bias_ref, latent_t_ref, proj_t_ref, latent_ref, gain_ref,
    hidden_ref, norm_ref, acc, peak_ref, total_ref,
):
    step = pl.program_id(0)
    width, rows = latent_t_ref.shape
    heads = peak_ref.shape[0]
    size = width // heads
    sources, capacity, channels = field_ref.shape
    half = capacity // 2
    pairs = sources * half

    @pl.when(step == 0)
    def start():
        acc[...] = jnp.zeros_like(acc)
        peak_ref[...] = jnp.zeros_like(peak_ref)
        total_ref[...] = jnp.ones_like(total_ref)

    member = lax.broadcasted_iota(jnp.int32, (rows, pairs), 0) == target_ref[0]
    chosen = jnp.where(member, 1.0, 0.0).astype(BF16)
    queries = jnp.dot(latent_t_ref[...], chosen, preferred_element_type=F32)
    scores, fields = [], []
    for parity in range(2):
        part = field_ref[:, parity * half : (parity + 1) * half, :].reshape(pairs, channels)
        keys = lax.dot_general(proj_t_ref[0:width, :], part, NT, preferred_element_type=F32)
        logits = jnp.sum((queries * keys).reshape(heads, size, pairs), axis=1)
        scores.append(logits * (size ** -0.5) + bias_ref[0, parity : parity + 1, :])
        fields.append(part)
    pair_peak = jnp.maximum(scores[0], scores[1])
    lane = lax.broadcasted_iota(jnp.int32, (rows, 128), 1)
    peaks = jnp.full((rows, 128), NEG, F32)
    for head in range(heads):
        column = jnp.max(
            jnp.where(member, pair_peak[head : head + 1, :], NEG), axis=1, keepdims=True
        )
        peaks = jnp.where(lane == head, column, peaks)
    block_peak = peaks.T[0:heads, :]
    old = peak_ref[...]
    new = jnp.maximum(old, block_peak)
    upper = new.astype(BF16)
    lower = (new - upper.astype(F32)).astype(BF16)
    new = upper.astype(F32) + lower.astype(F32)
    peak_ref[...] = new
    factor = jnp.exp(old - new)
    slot_peak = jnp.dot(upper, chosen, preferred_element_type=F32) + jnp.dot(
        lower, chosen, preferred_element_type=F32
    )
    weights = [jnp.exp(score - slot_peak) for score in scores]
    both = weights[0] + weights[1]
    both_upper = both.astype(BF16)
    both_lower = (both - both_upper.astype(F32)).astype(BF16)
    sums = lax.dot_general(both_upper, chosen, NT, preferred_element_type=F32)
    sums = sums + lax.dot_general(both_lower, chosen, NT, preferred_element_type=F32)
    total_ref[...] = total_ref[...] * factor + sums
    mixed = None
    for parity in range(2):
        values = lax.dot_general(
            proj_t_ref[width : 2 * width, :], fields[parity], NT, preferred_element_type=F32
        )
        term = values.reshape(heads, size, pairs) * weights[parity][:, None, :]
        mixed = term if mixed is None else mixed + term
    mixed = mixed.reshape(width, pairs).astype(BF16)
    added = lax.dot_general(mixed, chosen, NT, preferred_element_type=F32)
    acc[...] = (
        acc[...].reshape(heads, size, rows) * factor[:, None, :]
    ).reshape(width, rows) + added

    @pl.when(step == pl.num_programs(0) - 1)
    def finish():
        scale = 1.0 / total_ref[...]
        encoded = (acc[...].reshape(heads, size, rows) * scale[:, None, :]).reshape(width, rows)
        hidden = latent_ref[...].astype(F32) + encoded.T
        hidden_ref[...] = hidden
        center = hidden - jnp.mean(hidden, axis=1, keepdims=True)
        variance = jnp.mean(center * center, axis=1, keepdims=True)
        norm_ref[...] = (center * lax.rsqrt(variance + 1e-05) * gain_ref[...]).astype(BF16)


def attention_kernel(
    last, before_ref, norm_ref, after_ref, hidden_ref, proj_ref, table_ref, out_proj_ref,
    cotangent_ref, processed_ref, grad_ref, extended, pairs, queries, attended,
):
    device = lax.axis_index("seq")
    rows, width = norm_ref.shape
    heads = table_ref.shape[0]
    size = width // heads
    reach = before_ref.shape[0]
    span = 3 * reach
    extended[0:reach, :] = before_ref[...]
    extended[reach : reach + rows, :] = norm_ref[...]
    extended[reach + rows :, :] = after_ref[...]
    tile = 512

    def query_tile(index, carry):
        at = pl.ds(pl.multiple_of(index * tile, tile), tile)
        queries[:, at] = jnp.dot(
            norm_ref[...], proj_ref[:, at], preferred_element_type=F32
        ).astype(BF16)
        return carry

    lax.fori_loop(0, width // tile, query_tile, 0)

    def pair_tile(index, carry):
        at = pl.ds(pl.multiple_of(index * tile, tile), tile)
        here = pl.ds(pl.multiple_of(index * tile + width, tile), tile)
        pairs[:, at] = jnp.dot(
            extended[...], proj_ref[:, here], preferred_element_type=F32
        ).astype(BF16)
        return carry

    lax.fori_loop(0, 2 * width // tile, pair_tile, 0)
    key = lax.broadcasted_iota(jnp.int32, (1, span), 1)
    edges = [
        jnp.where((key < reach) & (device == 0), NEG, 0.0),
        jnp.where((key >= 2 * reach) & (device == last), NEG, 0.0),
    ]
    for head in range(heads):
        columns = slice(head * size, (head + 1) * size)
        value_columns = slice(width + head * size, width + (head + 1) * size)
        row = jnp.broadcast_to(table_ref[head : head + 1, :], (reach, span))
        table = pltpu.roll(row, 0, 1, stride=1, stride_axis=0)
        for block in range(2):
            mine = slice(block * reach, (block + 1) * reach)
            theirs = slice(block * reach, block * reach + span)
            logits = lax.dot_general(
                queries[mine, columns], pairs[theirs, columns], NT, preferred_element_type=F32
            )
            logits = logits * (size ** -0.5) + table + edges[block]
            powered = jnp.exp(logits - jnp.max(logits, axis=1, keepdims=True))
            total = jnp.sum(powered, axis=1, keepdims=True)
            probs = (powered / total).astype(BF16)
            mixture = jnp.dot(probs, pairs[theirs, value_columns], preferred_element_type=F32)
            attended[mine, columns] = mixture.astype(BF16)

    def out_tile(index, carry):
        at = pl.ds(pl.multiple_of(index * tile, tile), tile)
        processed_ref[:, at] = (
            hidden_ref[:, at]
            + jnp.dot(attended[...], out_proj_ref[:, at], preferred_element_type=F32)
        ).astype(BF16)
        return carry

    lax.fori_loop(0, width // tile, out_tile, 0)

    for group in range(X):
        part = lax.dot_general(
            attended[:, group * 256 : (group + 1) * 256], cotangent_ref[0], TN,
            preferred_element_type=F32,
        )
        grad_ref[group * 16 : (group + 1) * 16] = part.astype(BF16).reshape(16, 16, width)


def reduce_kernel(
    grad_ref, out_ref, from_core, merged, x_in, x_sum, z_in, y_all,
    v_in, v_sum, u_in, u_sum, w_in, r_all, send, recv,
):
    seq = lax.axis_index("seq")
    y = lax.axis_index("dp")
    core = seq % CORES
    z = (seq // CORES) % Z
    x = seq // (CORES * Z)

    def at(y_to, x_to, z_to, core_to):
        return (y_to, x_to * (Z * CORES) + z_to * CORES + core_to)

    sibling = at(y, x, z, 1 - core)
    x_peers = [at(y, (x + k) % X, z, core) for k in range(1, X)]
    y_peers = [at((y + k) % Y, x, z, core) for k in range(1, Y)]
    z_peers = [at(y, x, (z + k) % Z, core) for k in range(1, Z)]
    barrier = pltpu.get_barrier_semaphore()
    peers = [sibling] + x_peers + y_peers + z_peers
    for peer in peers:
        pl.semaphore_signal(barrier, inc=1, device_id=peer, device_id_type=MESH)
    pl.semaphore_wait(barrier, len(peers))

    count = iter(range(64))

    def copy(src, dst, peer):
        n = next(count)
        made = pltpu.make_async_remote_copy(
            src_ref=src, dst_ref=dst, send_sem=send.at[n], recv_sem=recv.at[n],
            device_id=peer, device_id_type=MESH,
        )
        made.start()
        return made

    half, quarter = 512, 128
    sent = []
    first = copy(
        grad_ref.at[:, 1 - core, :, 0:half], from_core.at[:, :, 0:half], sibling
    )
    second = copy(
        grad_ref.at[:, 1 - core, :, half:], from_core.at[:, :, half:], sibling
    )
    first.wait_recv()
    merged[:, :, 0:half] = (
        grad_ref[:, core, :, 0:half].astype(F32) + from_core[:, :, 0:half].astype(F32)
    ).astype(BF16)
    x_copies = [
        copy(merged.at[pl.ds(((x + k) % X) * Z, Z), :, 0:half], x_in.at[k - 1], x_peers[k - 1])
        for k in range(1, X)
    ]
    second.wait_recv()
    merged[:, :, half:] = (
        grad_ref[:, core, :, half:].astype(F32) + from_core[:, :, half:].astype(F32)
    ).astype(BF16)

    def strip(who):
        return pl.ds(pl.multiple_of(half + who * quarter, quarter), quarter)

    y_copies = [
        copy(merged.at[:, :, strip((y + k) % Y)], v_in.at[k - 1], y_peers[k - 1])
        for k in range(1, Y)
    ]

    for c in x_copies:
        c.wait_recv()
    x_sum[...] = (
        merged[pl.ds(x * Z, Z), :, 0:half].astype(F32)
        + (x_in[0].astype(F32) + x_in[1].astype(F32) + x_in[2].astype(F32))
    ).astype(BF16)
    z_copies = [
        copy(x_sum.at[(z + k) % Z], z_in.at[k - 1], z_peers[k - 1]) for k in range(1, Z)
    ]
    for c in y_copies:
        c.wait_recv()
    v_sum[...] = (
        merged[:, :, strip(y)].astype(F32)
        + (v_in[0].astype(F32) + v_in[1].astype(F32) + v_in[2].astype(F32))
    ).astype(BF16)
    u_copies = [
        copy(v_sum.at[pl.ds(((x + k) % X) * Z, Z)], u_in.at[k - 1], x_peers[k - 1])
        for k in range(1, X)
    ]
    for c in z_copies:
        c.wait_recv()
    part = x_sum[z].astype(F32)
    for k in range(Z - 1):
        part = part + z_in[k].astype(F32)
    y_all[y] = part
    s_copies = [copy(y_all.at[y], y_all.at[y], y_peers[k - 1]) for k in range(1, Y)]
    for c in u_copies:
        c.wait_recv()
    u_sum[...] = (
        v_sum[pl.ds(x * Z, Z)].astype(F32)
        + (u_in[0].astype(F32) + u_in[1].astype(F32) + u_in[2].astype(F32))
    ).astype(BF16)
    w_copies = [
        copy(u_sum.at[(z + k) % Z], w_in.at[k - 1], z_peers[k - 1]) for k in range(1, Z)
    ]
    for c in w_copies:
        c.wait_recv()
    part = u_sum[z].astype(F32)
    for k in range(Z - 1):
        part = part + w_in[k].astype(F32)
    r_all[y] = part
    r_copies = [copy(r_all.at[y], r_all.at[y], y_peers[k - 1]) for k in range(1, Y)]
    for c in s_copies:
        c.wait_recv()
    out_ref[:, 0:half] = (y_all[0] + y_all[1]) + (y_all[2] + y_all[3])
    for c in r_copies:
        c.wait_recv()
    for k in range(Y):
        out_ref[:, half + k * quarter : half + (k + 1) * quarter] = r_all[k]
    for c in [first, second] + x_copies + y_copies + z_copies + u_copies + s_copies + w_copies + r_copies:
        c.wait_send()


def shards(
    grid_fields, mesh_latent, edge_source, edge_target, edge_count, edge_bias, encoder_proj,
    norm_gain, processor_proj, offset_bias, windows, output_proj, cotangent,
):
    shard_count = lax.axis_size("seq")
    device = lax.axis_index("seq")
    rows, width = mesh_latent.shape
    heads = offset_bias.shape[0]
    reach = (offset_bias.shape[1] - 1) // 2
    channels, points = grid_fields.shape[1:]
    capacity = edge_source.shape[2]

    outgoing = pl.pallas_call(
        gather_kernel,
        out_shape=jax.ShapeDtypeStruct((shard_count, capacity, 128), BF16),
        in_specs=[pl.BlockSpec(memory_space=pltpu.SMEM), vmem()],
        out_specs=vmem(),
        scratch_shapes=[pltpu.VMEM((points, 128), F32), pltpu.VMEM((capacity, 128), F32)],
        compiler_params=pltpu.CompilerParams(vmem_limit_bytes=VMEM_LIMIT),
        name="take_fields",
    )(edge_source[0], grid_fields)
    incoming = lax.all_to_all(outgoing, "seq", split_axis=0, concat_axis=0, tiled=True)

    group = 8
    steps = shard_count // group
    pairs = group * capacity // 2
    own_counts = lax.dynamic_index_in_dim(edge_count, device, 1, keepdims=False)
    live = jnp.arange(capacity, dtype=jnp.int32)[None, :] < own_counts[:, None]
    bias = jnp.where(live, edge_bias[0], NEG)
    bias = bias.reshape(steps, pairs, 2).transpose(0, 2, 1)
    targets = edge_target[0].reshape(steps, pairs, 2)[:, :, 0].reshape(steps, 1, pairs)
    latent_t = mesh_latent.T
    proj_t = jnp.pad(encoder_proj, ((0, 128 - channels), (0, 0))).T
    offset = jnp.arange(3 * reach, dtype=jnp.int32) - reach
    table = jnp.where(
        jnp.abs(offset)[None, :] <= windows[:, None],
        jnp.pad(offset_bias, ((0, 0), (0, reach - 1))),
        NEG,
    )

    whole = lambda *shape: pl.BlockSpec(shape, lambda i: (0,) * len(shape))
    hidden, normalized = pl.pallas_call(
        edge_kernel,
        grid=(steps,),
        out_shape=(
            jax.ShapeDtypeStruct((rows, width), F32),
            jax.ShapeDtypeStruct((rows, width), BF16),
        ),
        in_specs=[
            pl.BlockSpec((group, capacity, 128), lambda i: (i, 0, 0)),
            pl.BlockSpec((1, 1, pairs), lambda i: (i, 0, 0)),
            pl.BlockSpec((1, 2, pairs), lambda i: (i, 0, 0)),
            whole(width, rows),
            whole(2 * width, 128),
            whole(rows, width),
            whole(1, width),
        ],
        out_specs=(whole(rows, width), whole(rows, width)),
        scratch_shapes=[
            pltpu.VMEM((width, rows), F32),
            pltpu.VMEM((heads, rows), F32),
            pltpu.VMEM((heads, rows), F32),
        ],
        compiler_params=pltpu.CompilerParams(vmem_limit_bytes=VMEM_LIMIT),
        name="attend_edges",
    )(incoming, targets, bias, latent_t, proj_t, mesh_latent, norm_gain[None])

    up = [(i, i + 1) for i in range(shard_count - 1)]
    down = [(j, i) for i, j in up]
    before = lax.ppermute(normalized[rows - reach :], "seq", up)
    after = lax.ppermute(normalized[:reach], "seq", down)

    processed, grad = pl.pallas_call(
        functools.partial(attention_kernel, shard_count - 1),
        out_shape=(
            jax.ShapeDtypeStruct((rows, width), BF16),
            jax.ShapeDtypeStruct((width // 16, 16, width), BF16),
        ),
        in_specs=[vmem()] * 8,
        out_specs=(vmem(), vmem()),
        scratch_shapes=[
            pltpu.VMEM((rows + 2 * reach, width), BF16),
            pltpu.VMEM((rows + 2 * reach, 2 * width), BF16),
            pltpu.VMEM((rows, width), BF16),
            pltpu.VMEM((rows, width), BF16),
        ],
        compiler_params=pltpu.CompilerParams(vmem_limit_bytes=VMEM_LIMIT),
        name="window_attention",
    )(before, normalized, after, hidden, processor_proj, table, output_proj, cotangent)

    gradient = pl.pallas_call(
        reduce_kernel,
        out_shape=jax.ShapeDtypeStruct((16, width), F32),
        in_specs=[vmem()],
        out_specs=vmem(),
        scratch_shapes=[
            pltpu.VMEM((32, 16, 1024), BF16),
            pltpu.VMEM((32, 16, 1024), BF16),
            pltpu.VMEM((3, 8, 16, 512), BF16),
            pltpu.VMEM((8, 16, 512), BF16),
            pltpu.VMEM((7, 16, 512), BF16),
            pltpu.VMEM((4, 16, 512), F32),
            pltpu.VMEM((3, 32, 16, 128), BF16),
            pltpu.VMEM((32, 16, 128), BF16),
            pltpu.VMEM((3, 8, 16, 128), BF16),
            pltpu.VMEM((8, 16, 128), BF16),
            pltpu.VMEM((7, 16, 128), BF16),
            pltpu.VMEM((4, 16, 128), F32),
            pltpu.SemaphoreType.DMA((64,)),
            pltpu.SemaphoreType.DMA((64,)),
        ],
        compiler_params=pltpu.CompilerParams(
            vmem_limit_bytes=VMEM_LIMIT, collective_id=1, has_side_effects=True
        ),
        name="reduce_gradient",
    )(grad.reshape(32, 2, 16, width))
    return (processed[None], gradient)


def solution(mesh):
    in_specs = (
        P("dp", None, "seq"),
        P("seq", None),
        P("seq", None, None),
        P("seq", None, None),
        P(),
        P("seq", None, None),
        P(),
        P(),
        P(),
        P(),
        P(),
        P(),
        P("dp", "seq", None),
    )
    out_specs = (P("dp", "seq", None), P("seq", None))
    return jax.shard_map(shards, mesh=mesh, in_specs=in_specs, out_specs=out_specs, check_vma=False)
```

time: 1130 us -> 176 us (0.16)
  local copies, waits for them, and re-layouts: 611 us -> 20.1 us
  waiting for transfers between devices: 269 us -> 36.6 us
  other arithmetic: 116 us -> 1.33 us
  Pallas kernels: 0 us -> 98.9 us
  matrix products: 94.5 us -> 0 us
  between operations: 14.3 us -> 0.73 us
    gather x12 -> x0, local copies, waits for them, and re-layouts: 567 us -> none  [the longest x2 469 us: window_attention(): jnp.take(offset_bias, jnp.clip(offset + reach, 0, 2 * reach), axis=1)]
    psum x1 -> x0, waiting for transfers between devices: 267 us -> none  [shards(): summed = lax.psum(local_grad, ('dp', 'seq'))]
    pallas_call x0 -> x4, Pallas kernels: none -> 98.9 us  [the longest x1 34 us: shards(): pl.pallas_call(reduce_kernel, out_shape=jax.ShapeDtypeStruct((16, width),...]
    dot_general x25 -> x0, matrix products: 94.5 us -> none  [the longest x4 36.4 us: source_step(): lax.dot_general(features, encoder_proj, (((0,), (0,)), ((), ())), preferr...]
    reduce_max x64 -> x0, other arithmetic: 45.5 us -> none  [head_max(): return jnp.max(jnp.where(member, column[:, None], -1e+30), axis=0)]
    all_to_all x1, waiting for transfers between devices: 0.01 us -> 33.6 us  [shards(): lax.all_to_all(outgoing, 'seq', split_axis=0, concat_axis=0, tiled=True)]
    reduce_sum x6 -> x0, other arithmetic: 27.9 us -> none  [the longest x4 24.9 us: attend_edges(): jnp.sum(queries * key_part, axis=-1) / math.sqrt(head_size)]
    convert_element_type x4 -> x0, other arithmetic: 17.6 us -> none  [attend_edges(): (weighted - upper_part.astype(jnp.float32)).astype(jnp.bfloat16)]
  transfers between devices with their start and end apart: 4 -> 3, of which waited for: 3 -> 3; matrix products, arithmetic and copies ran while one was open for 43% -> 10% of each run, Pallas kernels for 0% -> 0%
where the time goes in v1:
time: 176 us; the launch traced here: 175 us
  Pallas kernels  98.9 us (56%)
  waiting for transfers between devices  36.6 us (21%)
  local copies, waits for them, and re-layouts  20.1 us (11%)
  starting transfers between devices  17.5 us (10%)
    pallas_call x1, Pallas kernels, shards(): pl.pallas_call(reduce_kernel, out_shape=jax.ShapeDtypeStruct((16, width),...  34 us
    all_to_all x1, waiting for transfers between devices, shards(): lax.all_to_all(outgoing, 'seq', split_axis=0, concat_axis=0, tiled=True)  33.6 us
    pallas_call x1, Pallas kernels, shards(): pl.pallas_call(edge_kernel, grid=(steps,), out_shape=(jax.ShapeDtypeStruc...  29.1 us
    pallas_call x1, Pallas kernels, shards(): pl.pallas_call(functools.partial(attention_kernel, shard_count - 1), out_...  22.6 us
    pallas_call x1, Pallas kernels, shards(): pl.pallas_call(gather_kernel, out_shape=jax.ShapeDtypeStruct((shard_count...  13.2 us
    all_to_all x1, starting transfers between devices, shards(): lax.all_to_all(outgoing, 'seq', split_axis=0, concat_axis=0, tiled=True)  11.7 us
    unnamed x22, local copies, waits for them, and re-layouts  8.61 us
    squeeze x2, local copies, waits for them, and re-layouts, shards(): bias = jnp.where(live, edge_bias[0], NEG)  5.61 us
  transfers between devices with their start and end apart: 3, of which 3 were waited for; matrix products, arithmetic and copies ran while one was open for 10% of the time, Pallas kernels for 0%

profile of v1, /device:TPU:32, one launch (start us, length us, event | category | flops | bytes accessed | tf_op | source)
XLA Modules:
  0.0 175.1 jit_solution(15537061205397438343)
XLA Ops:
  0.6 0.0 copy-start
  0.6 13.2 %take_fields.1 = bf16[64,128,128]{2,1,0:T(8,128)(2,1)} custom-call(s32[64,128]{1,0:T(8,128)} %bitcast.17, bf16[1,100,4096]{2,1,0:T(8,128)(2,1)} %grid_ref.1), custom_call_target="tpu_custom_call" | custom-call | tf_op jit(solution)/shard_map/take_fields/pallas_call | solution.py:328
  13.8 11.7 %all-to-all-start = ((bf16[64,128,128]{2,1,0:T(8,128)(2,1)}), bf16[64,128,128]{2,1,0:T(8,128)(2,1)S(1)}, u32[]{:S(2)}, u32[]{:S(2)}) async-start(bf16[64,128,128]{2,1,0:T(8,128)(2,1)} %take_fields.1), calls=%async_computation | async-start | bytes 4194304 | tf_op jit(solution)/shard_map/all_to_all | solution.py:337
  25.6 0.0 copy-done
  25.6 0.2 dynamic-slice_reduce_fusion
  25.8 0.1 lt.41
  25.8 0.1 lt.42
  25.9 0.1 lt.43
  26.0 3.4 %squeeze.9 = f32[8,512,2]{2,1,0:T(8,128)} reshape(f32[1,64,128]{2,1,0:T(8,128)S(1)} %copy-done.5) | data formatting | bytes 65536 | tf_op jit(solution)/shard_map/squeeze | solution.py:344
  29.4 2.2 %copy.18 = f32[8,512,2]{1,2,0:T(2,128)S(1)} copy(f32[8,512,2]{2,1,0:T(8,128)} %squeeze.9) | data formatting | bytes 65536 | tf_op jit(solution)/shard_map/squeeze | solution.py:344
  31.6 0.1 lt.38
  31.7 0.0 copy-done.6
  31.7 3.4 %reshape_squeeze.6 = s32[8,512,2]{2,1,0:T(8,128)} reshape(s32[1,64,128]{2,1,0:T(8,128)S(1)} %copy-done.6) | data formatting | bytes 65536 | tf_op jit(solution)/shard_map/reshape;squeeze | solution.py:346
  35.1 2.8 %copy.21 = s32[8,512,1]{1,2,0:T(1,128)} copy(s32[8,512,1]{2,1,0:T(8,128)} %bitcast.13) | data formatting | bytes 32768
  37.9 1.3 copy.20
  39.2 1.0 copy.19
  40.2 0.6 fusion.bias_ref
  40.9 0.9 pad_bitcast_fusion.proj_t_ref
  41.8 33.6 %all-to-all-done.field_ref = bf16[64,128,128]{2,1,0:T(8,128)(2,1)S(1)} async-done(((bf16[64,128,128]{2,1,0:T(8,128)(2,1)}), bf16[64,128,128]{2,1,0:T(8,128)(2,1)S(1)}, u32[]{:S(2)}, u32[]{:S(2)}) %all-to-all-start) | async-done | bytes 2097184 | tf_op jit(solution)/shard_map/all_to_all | solution.py:337
  75.4 1.3 copy-done.1
  76.7 29.1 %attend_edges.1 = (f32[256,1024]{1,0:T(8,128)}, bf16[256,1024]{1,0:T(8,128)(2,1)}) custom-call(bf16[64,128,128]{2,1,0:T(8,128)(2,1)} %copy-done.1, s32[8,1,512]{2,1,0:T(1,128)} %bitcast.16, f32[8,2,512]{2,1,0:T(2,128)} %fusion.bias_ref, bf16[1024,256]{1,0:T(8,128)(2,1)} %bitcast.15, bf16[2048,128]{1,0:T(8,128)(2,1)} %pad_bitcast_fusion.proj_t_ref, ...), custom_call_target="tpu_custom_call" | custom-call | tf_op jit(solution)/shard_map/attend_edges/pallas_call | solution.py:357
  105.8 1.1 fusion.1
  106.8 2.2 %collective-permute-start = (bf16[128,1024]{1,0:T(8,128)(2,1)S(1)}, bf16[128,1024]{1,0:T(8,128)(2,1)S(1)}, u32[]{:S(2)}, u32[]{:S(2)}) collective-permute-start(bf16[128,1024]{1,0:T(8,128)(2,1)S(1)} %get-tuple-element.11), channel_id=1, source_target_pairs={{0,1},{1,2},{2,3},{3,4},{4,5},{5,6},{6,7},{7,8},{8,9},{9,10},{10,1... | collective-permute-start | bytes 786440 | tf_op jit(solution)/shard_map/ppermute | solution.py:385
  109.0 3.6 %collective-permute-start.1 = (bf16[128,1024]{1,0:T(8,128)(2,1)S(1)}, bf16[128,1024]{1,0:T(8,128)(2,1)S(1)}, u32[]{:S(2)}, u32[]{:S(2)}) collective-permute-start(bf16[128,1024]{1,0:T(8,128)(2,1)S(1)} %get-tuple-element.10), channel_id=1, source_target_pairs={{1,0},{2,1},{3,2},{4,3},{5,4},{6,5},{7,6},{8,7},{9,8},{10,9},{11,1... | collective-permute-start | bytes 786440 | tf_op jit(solution)/shard_map/ppermute | solution.py:386
  112.6 0.7 pad_select_fusion.table_ref
  113.3 1.2 collective-permute-done.before_ref
  114.5 1.8 %collective-permute-done.1.after_ref = bf16[128,1024]{1,0:T(8,128)(2,1)S(1)} collective-permute-done((bf16[128,1024]{1,0:T(8,128)(2,1)S(1)}, bf16[128,1024]{1,0:T(8,128)(2,1)S(1)}, u32[]{:S(2)}, u32[]{:S(2)}) %collective-permute-start.1) | collective-permute-done | bytes 262176 | tf_op jit(solution)/shard_map/ppermute | solution.py:386
  116.3 0.0 copy-done.3
  116.3 0.7 copy-done.4
  117.0 22.6 %window_attention.1 = (bf16[256,1024]{1,0:T(8,128)(2,1)}, bf16[64,16,1024]{2,1,0:T(8,128)(2,1)}) custom-call(bf16[128,1024]{1,0:T(8,128)(2,1)} %copy-done.3, bf16[256,1024]{1,0:T(8,128)(2,1)} %get-tuple-element.6.norm_ref, bf16[128,1024]{1,0:T(8,128)(2,1)} %copy-done.4, f32[256,1024]{1,0:T(8,128)} %get-tuple-element.7.hidden_ref, ...), custom_call_target="tpu_custom_call" | custom-call | tf_op jit(solution)/shard_map/window_attention/pallas_call | solution.py:388
  139.6 34.0 %reduce_gradient.1 = f32[16,1024]{1,0:T(8,128)} custom-call(bf16[32,2,16,1024]{3,2,1,0:T(8,128)(2,1)} %bitcast.14), custom_call_target="tpu_custom_call" | custom-call | tf_op jit(solution)/shard_map/reduce_gradient/pallas_call | solution.py:406
  173.6 1.5 copy.23
  (15 shorter events, 0.0 us)
Async XLA Ops:
  0.6 24.9 %copy-start = (s32[64,64]{1,0:T(8,128)S(1)}, s32[64,64]{1,0:T(8,128)}, u32[]{:S(2)}) copy-start(s32[64,64]{1,0:T(8,128)} %param.17) | copy-start | bytes 49156
  13.8 12.2 %copy-start.5 = (f32[1,64,128]{2,1,0:T(8,128)S(1)}, f32[1,64,128]{2,1,0:T(8,128)}, u32[]{:S(2)}) copy-start(f32[1,64,128]{2,1,0:T(8,128)} %param.18) | copy-start | bytes 98308
  13.8 61.5 %all-to-all-start = ((bf16[64,128,128]{2,1,0:T(8,128)(2,1)}), bf16[64,128,128]{2,1,0:T(8,128)(2,1)S(1)}, u32[]{:S(2)}, u32[]{:S(2)}) async-start(bf16[64,128,128]{2,1,0:T(8,128)(2,1)} %take_fields.1), calls=%async_computation | async-start | bytes 4194304 | tf_op jit(solution)/shard_map/all_to_all | solution.py:337
  26.0 5.7 %copy-start.6 = (s32[1,64,128]{2,1,0:T(8,128)S(1)}, s32[1,64,128]{2,1,0:T(8,128)}, u32[]{:S(2)}) copy-start(s32[1,64,128]{2,1,0:T(8,128)} %param.16) | copy-start | bytes 98308
  31.7 7.5 %copy-start.2 = (bf16[256,1024]{1,0:T(8,128)(2,1)S(1)}, bf16[256,1024]{1,0:T(8,128)(2,1)}, u32[]{:S(2)}) copy-start(bf16[256,1024]{1,0:T(8,128)(2,1)} %latent_ref.1) | copy-start | bytes 1572868
  75.4 1.3 copy-start.1
  76.7 35.9 %copy-start.7 = (f32[16,257]{1,0:T(8,128)S(1)}, f32[16,257]{1,0:T(8,128)}, u32[]{:S(2)}) copy-start(f32[16,257]{1,0:T(8,128)} %param.22) | copy-start | bytes 49348
  76.7 35.9 %copy-start.8 = (s32[16]{0:T(128)S(1)}, s32[16]{0:T(128)}, u32[]{:S(2)}) copy-start(s32[16]{0:T(128)} %param.23) | copy-start | bytes 196
  106.8 7.7 %collective-permute-start = (bf16[128,1024]{1,0:T(8,128)(2,1)S(1)}, bf16[128,1024]{1,0:T(8,128)(2,1)S(1)}, u32[]{:S(2)}, u32[]{:S(2)}) collective-permute-start(bf16[128,1024]{1,0:T(8,128)(2,1)S(1)} %get-tuple-element.11), channel_id=1, source_target_pairs={{0,1},{1,2},{2,3},{3,4},{4,5},{5,6},{6,7},{7,8},{8,9},{9,10},{10,1... | collective-permute-start | bytes 786440 | tf_op jit(solution)/shard_map/ppermute | solution.py:385
  109.0 7.2 %collective-permute-start.1 = (bf16[128,1024]{1,0:T(8,128)(2,1)S(1)}, bf16[128,1024]{1,0:T(8,128)(2,1)S(1)}, u32[]{:S(2)}, u32[]{:S(2)}) collective-permute-start(bf16[128,1024]{1,0:T(8,128)(2,1)S(1)} %get-tuple-element.10), channel_id=1, source_target_pairs={{1,0},{2,1},{3,2},{4,3},{5,4},{6,5},{7,6},{8,7},{9,8},{10,9},{11,1... | collective-permute-start | bytes 786440 | tf_op jit(solution)/shard_map/ppermute | solution.py:386
  114.5 1.8 %copy-start.3 = (bf16[128,1024]{1,0:T(8,128)(2,1)}, bf16[128,1024]{1,0:T(8,128)(2,1)S(1)}, u32[]{:S(2)}) copy-start(bf16[128,1024]{1,0:T(8,128)(2,1)S(1)} %collective-permute-done.before_ref) | copy-start | bytes 786436
  116.3 0.7 copy-start.4

commit v2 on v1

--- a/solution.py
+++ b/solution.py
@@ -22,105 +22,223 @@
     return pl.BlockSpec(memory_space=pltpu.VMEM)
 
 
-def gather_kernel(source_ref, grid_ref, out_ref, table, stage):
+def encode_kernel(
+    source_ref, grid_ref, target_ref, count_ref, bias_ref, latent_ref, proj_ref, gain_ref,
+    hidden_ref, norm_ref, table, stage, outgoing, incoming, latent_t, proj_t, counts,
+    targets, biases, acc, peak_ref, total_ref, send, recv,
+):
+    seq = lax.axis_index("seq")
+    y = lax.axis_index("dp")
+    core = seq % CORES
+    z = (seq // CORES) % Z
+    x = seq // (CORES * Z)
     channels = grid_ref.shape[1]
     owners, capacity = source_ref.shape
+    rows, width = latent_ref.shape
+    heads = peak_ref.shape[0]
+    size = width // heads
+    half = capacity // 2
+    group = 2 * X
+    depth = outgoing.shape[1]
+
+    def z_shift(turn):
+        return 4 + (1 - 2 * (turn % 2)) * ((turn + 1) // 2)
+
+    barrier = pltpu.get_barrier_semaphore()
+
+    def greet(offset, carry):
+        pl.semaphore_signal(
+            barrier, inc=1, device_id=(y, (seq + offset) % owners), device_id_type=MESH
+        )
+        return carry
+
+    lax.fori_loop(1, owners, greet, 0)
     stage[...] = jnp.zeros_like(stage)
 
-    def turn(chunk, carry):
+    def turn_fields(chunk, carry):
         start = pl.multiple_of(chunk * 128, 128)
         stage[0:channels, :] = grid_ref[0, :, pl.ds(start, 128)].astype(F32)
         table[pl.ds(start, 128), :] = stage[...].T
         return carry
 
-    lax.fori_loop(0, grid_ref.shape[2] // 128, turn, 0)
-
-    def owner_step(owner, carry):
+    lax.fori_loop(0, grid_ref.shape[2] // 128, turn_fields, 0)
+    pl.semaphore_wait(barrier, owners - 1)
+
+    def block_copy(step):
+        to_x = (x + (step // CORES) % X) % X
+        to_z = (z + z_shift(step // group)) % Z
+        to = to_x * (Z * CORES) + to_z * CORES + step % CORES
+        slot = step - step % CORES + core
+        copy = pltpu.make_async_remote_copy(
+            src_ref=outgoing.at[step], dst_ref=incoming.at[slot],
+            send_sem=send.at[step], recv_sem=recv.at[slot],
+            device_id=(y, to), device_id_type=MESH,
+        )
+        return to, copy
+
+    def send_step(step, carry):
+        to, copy = block_copy(step)
         for slot in range(capacity):
-            row = (slot % 2) * (capacity // 2) + slot // 2
-            stage[row : row + 1, :] = table[pl.ds(source_ref[owner, slot], 1), :]
-        out_ref[owner] = stage[...].astype(BF16)
-        return carry
-
-    lax.fori_loop(0, owners, owner_step, 0)
-
-
-def edge_kernel(
-    field_ref, target_ref, bias_ref, latent_t_ref, proj_t_ref, latent_ref, gain_ref,
-    hidden_ref, norm_ref, acc, peak_ref, total_ref,
-):
-    step = pl.program_id(0)
-    width, rows = latent_t_ref.shape
-    heads = peak_ref.shape[0]
-    size = width // heads
-    sources, capacity, channels = field_ref.shape
-    half = capacity // 2
-    pairs = sources * half
-
-    @pl.when(step == 0)
-    def start():
-        acc[...] = jnp.zeros_like(acc)
-        peak_ref[...] = jnp.zeros_like(peak_ref)
-        total_ref[...] = jnp.ones_like(total_ref)
-
-    member = lax.broadcasted_iota(jnp.int32, (rows, pairs), 0) == target_ref[0]
-    chosen = jnp.where(member, 1.0, 0.0).astype(BF16)
-    queries = jnp.dot(latent_t_ref[...], chosen, preferred_element_type=F32)
-    scores, fields = [], []
+            row = (slot % 2) * half + slot // 2
+            stage[row : row + 1, :] = table[pl.ds(source_ref[to, slot], 1), :]
+        block = stage[...].T[0:depth, :].astype(BF16)
+
+        @pl.when(to == seq)
+        def keep():
+            incoming[step] = block
+
+        @pl.when(to != seq)
+        def pass_on():
+            outgoing[step] = block
+            copy.start()
+
+        return carry
+
+    lax.fori_loop(0, owners, send_step, 0)
+
+    for chunk in range(width // 128):
+        here = slice(chunk * 128, (chunk + 1) * 128)
+        latent_t[here, :] = latent_ref[:, here].astype(F32).T.astype(BF16)
+    stage[...] = jnp.zeros_like(stage)
+
+    def turn_proj(chunk, carry):
+        start = pl.multiple_of(chunk * 128, 128)
+        stage[0:channels, :] = proj_ref[:, pl.ds(start, 128)].astype(F32)
+        proj_t[pl.ds(start, 128), :] = stage[...].T.astype(BF16)
+        return carry
+
+    lax.fori_loop(0, 2 * width // 128, turn_proj, 0)
+
+    chips = owners // CORES
+    lane = lax.broadcasted_iota(jnp.int32, (chips, capacity), 1)
+    slot_row = lax.broadcasted_iota(jnp.int32, (capacity, capacity), 0)
+    slot_lane = lax.broadcasted_iota(jnp.int32, (capacity, capacity), 1)
+    owner_lane = lax.broadcasted_iota(jnp.int32, (owners, owners), 1)
+    own = jnp.sum(jnp.where(owner_lane == seq, count_ref[...], 0), axis=1, keepdims=True)
+    counts[...] = jnp.broadcast_to(own, (owners, capacity))
+
+    def of_core(ref, which):
+        return ref[pl.ds(which, chips, stride=CORES), :]
+
+    def picks(parity, which):
+        wanted = slot_row == 2 * (slot_lane - which * half) + parity
+        in_half = (slot_lane >= which * half) & (slot_lane < (which + 1) * half)
+        return jnp.where(wanted & in_half, 1.0, 0.0)
+
+    found = jnp.zeros((chips, capacity), F32)
+    for which in range(CORES):
+        found = found + jnp.dot(
+            of_core(target_ref, which).astype(F32), picks(0, which),
+            precision=lax.Precision.HIGHEST, preferred_element_type=F32,
+        )
+    targets[...] = found.astype(jnp.int32)
+    live = jnp.where(lane < half, of_core(counts, 0), of_core(counts, 1))
     for parity in range(2):
-        part = field_ref[:, parity * half : (parity + 1) * half, :].reshape(pairs, channels)
-        keys = lax.dot_general(proj_t_ref[0:width, :], part, NT, preferred_element_type=F32)
-        logits = jnp.sum((queries * keys).reshape(heads, size, pairs), axis=1)
-        scores.append(logits * (size ** -0.5) + bias_ref[0, parity : parity + 1, :])
-        fields.append(part)
-    pair_peak = jnp.maximum(scores[0], scores[1])
-    lane = lax.broadcasted_iota(jnp.int32, (rows, 128), 1)
-    peaks = jnp.full((rows, 128), NEG, F32)
-    for head in range(heads):
-        column = jnp.max(
-            jnp.where(member, pair_peak[head : head + 1, :], NEG), axis=1, keepdims=True
+        found = jnp.zeros((chips, capacity), F32)
+        for which in range(CORES):
+            found = found + jnp.dot(
+                of_core(bias_ref, which), picks(parity, which),
+                precision=lax.Precision.HIGHEST, preferred_element_type=F32,
+            )
+        biases[parity] = jnp.where(2 * (lane % half) + parity < live, found, NEG)
+
+    acc[...] = jnp.zeros_like(acc)
+    peak_ref[...] = jnp.zeros_like(peak_ref)
+    total_ref[...] = jnp.ones_like(total_ref)
+    pairs = X * capacity
+    low = lax.broadcasted_iota(jnp.int32, (depth, capacity), 1) < half
+    peak_lane = lax.broadcasted_iota(jnp.int32, (rows, 128), 1)
+    row_index = lax.broadcasted_iota(jnp.int32, (rows, pairs), 0)
+
+    def group_step(turn, carry):
+        for member_at in range(group):
+            slot = turn * group + member_at
+
+            @pl.when(slot != (Z - 1) * group + core)
+            def arrive():
+                pltpu.make_async_copy(
+                    incoming.at[slot], incoming.at[slot], recv.at[slot]
+                ).wait()
+
+        evens, odds, rows_of, bias_of = [], [], [], [[], []]
+        for shift in range(X):
+            first = incoming[turn * group + CORES * shift].astype(F32)
+            second = incoming[turn * group + CORES * shift + 1].astype(F32)
+            evens.append(jnp.where(low, first, pltpu.roll(second, half, 1)).astype(BF16))
+            odds.append(jnp.where(low, pltpu.roll(first, half, 1), second).astype(BF16))
+            chip = ((x + X - shift) % X) * Z + (z + Z - z_shift(turn)) % Z
+            rows_of.append(targets[pl.ds(chip, 1), :])
+            for parity in range(2):
+                bias_of[parity].append(biases[parity, pl.ds(chip, 1), :])
+        target = jnp.concatenate(rows_of, axis=1)
+        member = row_index == target
+        chosen = jnp.where(member, 1.0, 0.0).astype(BF16)
+        queries = jnp.dot(latent_t[...], chosen, preferred_element_type=F32)
+        scores, fields = [], []
+        for parity, parts in enumerate((evens, odds)):
+            part = jnp.concatenate(parts, axis=1)
+            keys = jnp.dot(proj_t[0:width, 0:depth], part, preferred_element_type=F32)
+            logits = jnp.sum((queries * keys).reshape(heads, size, pairs), axis=1)
+            scores.append(logits * (size ** -0.5) + jnp.concatenate(bias_of[parity], axis=1))
+            fields.append(part)
+        pair_peak = jnp.maximum(scores[0], scores[1])
+        peaks = jnp.full((rows, 128), NEG, F32)
+        for head in range(heads):
+            column = jnp.max(
+                jnp.where(member, pair_peak[head : head + 1, :], NEG), axis=1, keepdims=True
+            )
+            peaks = jnp.where(peak_lane == head, column, peaks)
+        old = peak_ref[...]
+        new = jnp.maximum(old, peaks.T[0:heads, :])
+        upper = new.astype(BF16)
+        lower = (new - upper.astype(F32)).astype(BF16)
+        new = upper.astype(F32) + lower.astype(F32)
+        peak_ref[...] = new
+        factor = jnp.exp(old - new)
+        slot_peak = jnp.dot(upper, chosen, preferred_element_type=F32) + jnp.dot(
+            lower, chosen, preferred_element_type=F32
         )
-        peaks = jnp.where(lane == head, column, peaks)
-    block_peak = peaks.T[0:heads, :]
-    old = peak_ref[...]
-    new = jnp.maximum(old, block_peak)
-    upper = new.astype(BF16)
-    lower = (new - upper.astype(F32)).astype(BF16)
-    new = upper.astype(F32) + lower.astype(F32)
-    peak_ref[...] = new
-    factor = jnp.exp(old - new)
-    slot_peak = jnp.dot(upper, chosen, preferred_element_type=F32) + jnp.dot(
-        lower, chosen, preferred_element_type=F32
-    )
-    weights = [jnp.exp(score - slot_peak) for score in scores]
-    both = weights[0] + weights[1]
-    both_upper = both.astype(BF16)
-    both_lower = (both - both_upper.astype(F32)).astype(BF16)
-    sums = lax.dot_general(both_upper, chosen, NT, preferred_element_type=F32)
-    sums = sums + lax.dot_general(both_lower, chosen, NT, preferred_element_type=F32)
-    total_ref[...] = total_ref[...] * factor + sums
-    mixed = None
-    for parity in range(2):
-        values = lax.dot_general(
-            proj_t_ref[width : 2 * width, :], fields[parity], NT, preferred_element_type=F32
-        )
-        term = values.reshape(heads, size, pairs) * weights[parity][:, None, :]
-        mixed = term if mixed is None else mixed + term
-    mixed = mixed.reshape(width, pairs).astype(BF16)
-    added = lax.dot_general(mixed, chosen, NT, preferred_element_type=F32)
-    acc[...] = (
-        acc[...].reshape(heads, size, rows) * factor[:, None, :]
-    ).reshape(width, rows) + added
-
-    @pl.when(step == pl.num_programs(0) - 1)
-    def finish():
-        scale = 1.0 / total_ref[...]
-        encoded = (acc[...].reshape(heads, size, rows) * scale[:, None, :]).reshape(width, rows)
-        hidden = latent_ref[...].astype(F32) + encoded.T
-        hidden_ref[...] = hidden
-        center = hidden - jnp.mean(hidden, axis=1, keepdims=True)
-        variance = jnp.mean(center * center, axis=1, keepdims=True)
-        norm_ref[...] = (center * lax.rsqrt(variance + 1e-05) * gain_ref[...]).astype(BF16)
+        weights = [jnp.exp(score - slot_peak) for score in scores]
+        both = weights[0] + weights[1]
+        both_upper = both.astype(BF16)
+        both_lower = (both - both_upper.astype(F32)).astype(BF16)
+        sums = lax.dot_general(both_upper, chosen, NT, preferred_element_type=F32)
+        sums = sums + lax.dot_general(both_lower, chosen, NT, preferred_element_type=F32)
+        total_ref[...] = total_ref[...] * factor + sums
+        mixed = None
+        for parity in range(2):
+            values = jnp.dot(
+                proj_t[width : 2 * width, 0:depth], fields[parity], preferred_element_type=F32
+            )
+            term = values.reshape(heads, size, pairs) * weights[parity][:, None, :]
+            mixed = term if mixed is None else mixed + term
+        mixed = mixed.reshape(width, pairs).astype(BF16)
+        added = lax.dot_general(mixed, chosen, NT, preferred_element_type=F32)
+        acc[...] = (
+            acc[...].reshape(heads, size, rows) * factor[:, None, :]
+        ).reshape(width, rows) + added
+        return carry
+
+    lax.fori_loop(0, Z, group_step, 0)
+
+    scale = 1.0 / total_ref[...]
+    encoded = (acc[...].reshape(heads, size, rows) * scale[:, None, :]).reshape(width, rows)
+    hidden = latent_ref[...].astype(F32) + encoded.T
+    hidden_ref[...] = hidden
+    center = hidden - jnp.mean(hidden, axis=1, keepdims=True)
+    variance = jnp.mean(center * center, axis=1, keepdims=True)
+    norm_ref[...] = (center * lax.rsqrt(variance + 1e-05) * gain_ref[...]).astype(BF16)
+
+    def sent_step(step, carry):
+        to, copy = block_copy(step)
+
+        @pl.when(to != seq)
+        def done():
+            copy.wait_send()
+
+        return carry
+
+    lax.fori_loop(0, owners, sent_step, 0)
 
 
 def attention_kernel(
@@ -324,61 +442,45 @@
     reach = (offset_bias.shape[1] - 1) // 2
     channels, points = grid_fields.shape[1:]
     capacity = edge_source.shape[2]
-
-    outgoing = pl.pallas_call(
-        gather_kernel,
-        out_shape=jax.ShapeDtypeStruct((shard_count, capacity, 128), BF16),
-        in_specs=[pl.BlockSpec(memory_space=pltpu.SMEM), vmem()],
-        out_specs=vmem(),
-        scratch_shapes=[pltpu.VMEM((points, 128), F32), pltpu.VMEM((capacity, 128), F32)],
-        compiler_params=pltpu.CompilerParams(vmem_limit_bytes=VMEM_LIMIT),
-        name="take_fields",
-    )(edge_source[0], grid_fields)
-    incoming = lax.all_to_all(outgoing, "seq", split_axis=0, concat_axis=0, tiled=True)
-
-    group = 8
-    steps = shard_count // group
-    pairs = group * capacity // 2
-    own_counts = lax.dynamic_index_in_dim(edge_count, device, 1, keepdims=False)
-    live = jnp.arange(capacity, dtype=jnp.int32)[None, :] < own_counts[:, None]
-    bias = jnp.where(live, edge_bias[0], NEG)
-    bias = bias.reshape(steps, pairs, 2).transpose(0, 2, 1)
-    targets = edge_target[0].reshape(steps, pairs, 2)[:, :, 0].reshape(steps, 1, pairs)
-    latent_t = mesh_latent.T
-    proj_t = jnp.pad(encoder_proj, ((0, 128 - channels), (0, 0))).T
     offset = jnp.arange(3 * reach, dtype=jnp.int32) - reach
     table = jnp.where(
         jnp.abs(offset)[None, :] <= windows[:, None],
         jnp.pad(offset_bias, ((0, 0), (0, reach - 1))),
         NEG,
     )
-
-    whole = lambda *shape: pl.BlockSpec(shape, lambda i: (0,) * len(shape))
+    depth = (channels + 15) // 16 * 16
     hidden, normalized = pl.pallas_call(
-        edge_kernel,
-        grid=(steps,),
+        encode_kernel,
         out_shape=(
             jax.ShapeDtypeStruct((rows, width), F32),
             jax.ShapeDtypeStruct((rows, width), BF16),
         ),
-        in_specs=[
-            pl.BlockSpec((group, capacity, 128), lambda i: (i, 0, 0)),
-            pl.BlockSpec((1, 1, pairs), lambda i: (i, 0, 0)),
-            pl.BlockSpec((1, 2, pairs), lambda i: (i, 0, 0)),
-            whole(width, rows),
-            whole(2 * width, 128),
-            whole(rows, width),
-            whole(1, width),
-        ],
-        out_specs=(whole(rows, width), whole(rows, width)),
+        in_specs=[pl.BlockSpec(memory_space=pltpu.SMEM)] + [vmem()] * 7,
+        out_specs=(vmem(), vmem()),
         scratch_shapes=[
+            pltpu.VMEM((points, 128), F32),
+            pltpu.VMEM((128, 128), F32),
+            pltpu.VMEM((shard_count, depth, capacity), BF16),
+            pltpu.VMEM((shard_count, depth, capacity), BF16),
+            pltpu.VMEM((width, rows), BF16),
+            pltpu.VMEM((2 * width, 128), BF16),
+            pltpu.VMEM((shard_count, capacity), jnp.int32),
+            pltpu.VMEM((shard_count // CORES, capacity), jnp.int32),
+            pltpu.VMEM((2, shard_count // CORES, capacity), F32),
             pltpu.VMEM((width, rows), F32),
             pltpu.VMEM((heads, rows), F32),
             pltpu.VMEM((heads, rows), F32),
+            pltpu.SemaphoreType.DMA((shard_count,)),
+            pltpu.SemaphoreType.DMA((shard_count,)),
         ],
-        compiler_params=pltpu.CompilerParams(vmem_limit_bytes=VMEM_LIMIT),
-        name="attend_edges",
-    )(incoming, targets, bias, latent_t, proj_t, mesh_latent, norm_gain[None])
+        compiler_params=pltpu.CompilerParams(
+            vmem_limit_bytes=VMEM_LIMIT, collective_id=2, has_side_effects=True
+        ),
+        name="encode",
+    )(
+        edge_source[0], grid_fields, edge_target[0], edge_count, edge_bias[0], mesh_latent,
+        encoder_proj, norm_gain[None],
+    )
 
     up = [(i, i + 1) for i in range(shard_count - 1)]
     down = [(j, i) for i, j in up]

time: 176 us -> 141 us (0.80)
  waiting for transfers between devices: 36.6 us -> 4.87 us
  Pallas kernels: 98.9 us -> 126 us
  local copies, waits for them, and re-layouts: 20.1 us -> 3.24 us
  starting transfers between devices: 17.5 us -> 4.68 us
    all_to_all x1 -> x0, waiting for transfers between devices: 33.6 us -> none  [shards(): lax.all_to_all(outgoing, 'seq', split_axis=0, concat_axis=0, tiled=True)]
    pallas_call x2 -> x1, Pallas kernels: 42.3 us -> 69 us  [shards(): pl.pallas_call(encode_kernel, out_shape=(jax.ShapeDtypeStruct((rows, widt...]
    all_to_all x1 -> x0, starting transfers between devices: 11.7 us -> none  [shards(): lax.all_to_all(outgoing, 'seq', split_axis=0, concat_axis=0, tiled=True)]
    unnamed x22 -> x9, local copies, waits for them, and re-layouts: 8.61 us -> 2.17 us
    squeeze x2 -> x0, local copies, waits for them, and re-layouts: 5.61 us -> none  [shards(): bias = jnp.where(live, edge_bias[0], NEG)]
    another operation x1 -> x0, local copies, waits for them, and re-layouts: 3.41 us -> none  [shards(): edge_target[0].reshape(steps, pairs, 2)[:, :, 0].reshape(steps, 1, pairs)]
    ppermute x1, waiting for transfers between devices: 1.22 us -> 3.82 us  [shards(): before = lax.ppermute(normalized[rows - reach:], 'seq', up)]
  transfers between devices with their start and end apart: 3 -> 2, of which waited for: 3 -> 2; matrix products, arithmetic and copies ran while one was open for 10% -> 0% of each run, Pallas kernels for 0% -> 0%
where the time goes in v2:
time: 141 us; the launch traced here: 140 us
  Pallas kernels  126 us (89%)
  waiting for transfers between devices  4.87 us (3%)
  starting transfers between devices  4.68 us (3%)
  local copies, waits for them, and re-layouts  3.24 us (2%)
    pallas_call x1, Pallas kernels, shards(): pl.pallas_call(encode_kernel, out_shape=(jax.ShapeDtypeStruct((rows, widt...  69 us
    pallas_call x1, Pallas kernels, shards(): pl.pallas_call(reduce_kernel, out_shape=jax.ShapeDtypeStruct((16, width),...  34 us
    pallas_call x1, Pallas kernels, shards(): pl.pallas_call(functools.partial(attention_kernel, shard_count - 1), out_...  22.6 us
    ppermute x1, waiting for transfers between devices, shards(): before = lax.ppermute(normalized[rows - reach:], 'seq', up)  3.82 us
  transfers between devices with their start and end apart: 2, of which 2 were waited for; matrix products, arithmetic and copies ran while one was open for 0% of the time, Pallas kernels for 0%

profile of v2, /device:TPU:32, one launch (start us, length us, event | category | flops | bytes accessed | tf_op | source)
XLA Modules:
  0.0 139.8 jit_solution(4458174422305140399)
XLA Ops:
  0.6 0.0 copy-start.3
  0.6 0.0 copy-start.2
  0.7 69.0 %encode.1 = (f32[256,1024]{1,0:T(8,128)}, bf16[256,1024]{1,0:T(8,128)(2,1)}) custom-call(s32[64,128]{1,0:T(8,128)} %bitcast.7, bf16[1,100,4096]{2,1,0:T(8,128)(2,1)} %grid_ref.1, s32[64,128]{1,0:T(8,128)} %bitcast.8, s32[64,64]{1,0:T(8,128)} %count_ref.1, f32[64,128]{1,0:T(8,128)} %bitcast.9, bf16[256,1024]{1,0:T(8,128)(2,1)} %latent_ref.1, ...), custom_call_target="tpu_custom_call" | custom-call | tf_op jit(solution)/shard_map/encode/pallas_call | solution.py:452
  69.6 1.1 fusion
  70.7 2.6 %collective-permute-start.1 = (bf16[128,1024]{1,0:T(8,128)(2,1)S(1)}, bf16[128,1024]{1,0:T(8,128)(2,1)S(1)}, u32[]{:S(2)}, u32[]{:S(2)}) collective-permute-start(bf16[128,1024]{1,0:T(8,128)(2,1)S(1)} %get-tuple-element.10), channel_id=1, source_target_pairs={{1,0},{2,1},{3,2},{4,3},{5,4},{6,5},{7,6},{8,7},{9,8},{10,9},{11,1... | collective-permute-start | bytes 786440 | tf_op jit(solution)/shard_map/ppermute | solution.py:488
  73.3 2.1 %collective-permute-start = (bf16[128,1024]{1,0:T(8,128)(2,1)S(1)}, bf16[128,1024]{1,0:T(8,128)(2,1)S(1)}, u32[]{:S(2)}, u32[]{:S(2)}) collective-permute-start(bf16[128,1024]{1,0:T(8,128)(2,1)S(1)} %get-tuple-element.11), channel_id=1, source_target_pairs={{0,1},{1,2},{2,3},{3,4},{4,5},{5,6},{6,7},{7,8},{8,9},{9,10},{10,1... | collective-permute-start | bytes 786440 | tf_op jit(solution)/shard_map/ppermute | solution.py:487
  75.4 0.0 copy-done.3
  75.4 0.0 copy-done.2
  75.4 0.7 pad_select_fusion.table_ref
  76.1 1.0 collective-permute-done.1.after_ref
  77.2 0.0 copy-start
  77.2 3.8 %collective-permute-done.before_ref = bf16[128,1024]{1,0:T(8,128)(2,1)S(1)} collective-permute-done((bf16[128,1024]{1,0:T(8,128)(2,1)S(1)}, bf16[128,1024]{1,0:T(8,128)(2,1)S(1)}, u32[]{:S(2)}, u32[]{:S(2)}) %collective-permute-start) | collective-permute-done | bytes 262176 | tf_op jit(solution)/shard_map/ppermute | solution.py:487
  81.0 0.0 copy-start.1
  81.0 0.0 copy-done
  81.0 0.7 copy-done.1
  81.7 22.6 %window_attention.1 = (bf16[256,1024]{1,0:T(8,128)(2,1)}, bf16[64,16,1024]{2,1,0:T(8,128)(2,1)}) custom-call(bf16[128,1024]{1,0:T(8,128)(2,1)} %copy-done.1, bf16[256,1024]{1,0:T(8,128)(2,1)} %get-tuple-element.6.norm_ref, bf16[128,1024]{1,0:T(8,128)(2,1)} %copy-done, f32[256,1024]{1,0:T(8,128)} %get-tuple-element.7.hidden_ref, bf16[1024,3072]{1,0:T(8,128)(2,1)} %proj_ref.3, ...), custom_call_target="tpu_custom_call" | custom-call | tf_op jit(solution)/shard_map/window_attention/pallas_call | solution.py:490
  104.3 34.0 %reduce_gradient.1 = f32[16,1024]{1,0:T(8,128)} custom-call(bf16[32,2,16,1024]{3,2,1,0:T(8,128)(2,1)} %bitcast.6), custom_call_target="tpu_custom_call" | custom-call | tf_op jit(solution)/shard_map/reduce_gradient/pallas_call | solution.py:508
  138.3 1.5 %copy.16 = f32[16,1024]{1,0:T(8,128)} copy(f32[16,1024]{1,0:T(8,128)} %reduce_gradient.1) | data formatting | bytes 131072
  (1 shorter events, 0.0 us)
Async XLA Ops:
  0.6 74.8 %copy-start.3 = (s32[16]{0:T(128)S(1)}, s32[16]{0:T(128)}, u32[]{:S(2)}) copy-start(s32[16]{0:T(128)} %param.23) | copy-start | bytes 196
  0.6 74.8 %copy-start.2 = (f32[16,257]{1,0:T(8,128)S(1)}, f32[16,257]{1,0:T(8,128)}, u32[]{:S(2)}) copy-start(f32[16,257]{1,0:T(8,128)} %param.22) | copy-start | bytes 49348
  70.7 6.5 %collective-permute-start.1 = (bf16[128,1024]{1,0:T(8,128)(2,1)S(1)}, bf16[128,1024]{1,0:T(8,128)(2,1)S(1)}, u32[]{:S(2)}, u32[]{:S(2)}) collective-permute-start(bf16[128,1024]{1,0:T(8,128)(2,1)S(1)} %get-tuple-element.10), channel_id=1, source_target_pairs={{1,0},{2,1},{3,2},{4,3},{5,4},{6,5},{7,6},{8,7},{9,8},{10,9},{11,1... | collective-permute-start | bytes 786440 | tf_op jit(solution)/shard_map/ppermute | solution.py:488
  73.3 7.7 %collective-permute-start = (bf16[128,1024]{1,0:T(8,128)(2,1)S(1)}, bf16[128,1024]{1,0:T(8,128)(2,1)S(1)}, u32[]{:S(2)}, u32[]{:S(2)}) collective-permute-start(bf16[128,1024]{1,0:T(8,128)(2,1)S(1)} %get-tuple-element.11), channel_id=1, source_target_pairs={{0,1},{1,2},{2,3},{3,4},{4,5},{5,6},{6,7},{7,8},{8,9},{9,10},{10,1... | collective-permute-start | bytes 786440 | tf_op jit(solution)/shard_map/ppermute | solution.py:487
  77.2 3.8 %copy-start = (bf16[128,1024]{1,0:T(8,128)(2,1)}, bf16[128,1024]{1,0:T(8,128)(2,1)S(1)}, u32[]{:S(2)}) copy-start(bf16[128,1024]{1,0:T(8,128)(2,1)S(1)} %collective-permute-done.1.after_ref) | copy-start | bytes 786436
  81.0 0.7 copy-start.1

commit v3 on v2

v3 whole, which is shorter than its diff:
```python
import jax
import jax.numpy as jnp
from jax import lax
from jax.experimental import pallas as pl
from jax.experimental.pallas import tpu as pltpu
from jax.sharding import PartitionSpec as P

MESH = pl.DeviceIdType.MESH
X, Z, CORES, Y = 4, 8, 2, 4
NEG = -1e30
F32 = jnp.float32
BF16 = jnp.bfloat16
VMEM_LIMIT = 56 * 1024 * 1024

NT = (((1,), (1,)), ((), ()))
TN = (((0,), (0,)), ((), ()))


def vmem():
    return pl.BlockSpec(memory_space=pltpu.VMEM)


def layer_kernel(
    source_ref, grid_ref, target_ref, count_ref, bias_ref, latent_ref, proj_ref, gain_ref,
    offset_ref, big_hbm, out_hbm, cotangent_hbm,
    processed_ref, gradient_ref, table, stage, outgoing, incoming, latent_t, proj_t, counts,
    targets, biases, acc, peak_ref, total_ref, send, recv,
    big, out_proj, cotangent, fetched, hidden_ref, extended, mixed_rows, tables, attended,
    halo_send, halo_recv, grads, from_core, merged, x_in, x_sum, z_in, y_all, v_in, v_sum,
    u_in, u_sum, w_in, r_all, core_send, core_recv, x_send, x_recv, y_send, y_recv, z_send,
    z_recv, s_send, s_recv, u_send, u_recv, w_send, w_recv, r_send, r_recv,
):
    seq = lax.axis_index("seq")
    y = lax.axis_index("dp")
    core = seq % CORES
    z = (seq // CORES) % Z
    x = seq // (CORES * Z)
    channels = grid_ref.shape[1]
    owners, capacity = source_ref.shape
    rows, width = latent_ref.shape
    heads = peak_ref.shape[0]
    size = width // heads
    half = capacity // 2
    group = 2 * X
    depth = outgoing.shape[1]

    def z_shift(turn):
        return 4 + (1 - 2 * (turn % 2)) * ((turn + 1) // 2)

    barrier = pltpu.get_barrier_semaphore()

    def greet(offset, carry):
        pl.semaphore_signal(
            barrier, inc=1, device_id=(y, (seq + offset) % owners), device_id_type=MESH
        )
        return carry

    lax.fori_loop(1, owners, greet, 0)
    y_peers = [((y + k) % Y, seq) for k in range(1, Y)]
    for peer in y_peers:
        pl.semaphore_signal(barrier, inc=1, device_id=peer, device_id_type=MESH)
    fetches = [
        pltpu.make_async_copy(big_hbm, big, fetched.at[0]),
        pltpu.make_async_copy(out_hbm, out_proj, fetched.at[1]),
        pltpu.make_async_copy(cotangent_hbm, cotangent, fetched.at[2]),
    ]
    for fetch in fetches:
        fetch.start()
    stage[...] = jnp.zeros_like(stage)

    def turn_fields(chunk, carry):
        start = pl.multiple_of(chunk * 128, 128)
        stage[0:channels, :] = grid_ref[0, :, pl.ds(start, 128)].astype(F32)
        table[pl.ds(start, 128), :] = stage[...].T
        return carry

    lax.fori_loop(0, grid_ref.shape[2] // 128, turn_fields, 0)
    pl.semaphore_wait(barrier, owners - 1 + Y - 1)

    def block_copy(step):
        to_x = (x + (step // CORES) % X) % X
        to_z = (z + z_shift(step // group)) % Z
        to = to_x * (Z * CORES) + to_z * CORES + step % CORES
        slot = step - step % CORES + core
        copy = pltpu.make_async_remote_copy(
            src_ref=outgoing.at[step], dst_ref=incoming.at[slot],
            send_sem=send.at[step], recv_sem=recv.at[slot],
            device_id=(y, to), device_id_type=MESH,
        )
        return to, copy

    def send_step(step, carry):
        to, copy = block_copy(step)
        for slot in range(capacity):
            row = (slot % 2) * half + slot // 2
            stage[row : row + 1, :] = table[pl.ds(source_ref[to, slot], 1), :]
        block = stage[...].T[0:depth, :].astype(BF16)

        @pl.when(to == seq)
        def keep():
            incoming[step] = block

        @pl.when(to != seq)
        def pass_on():
            outgoing[step] = block
            copy.start()

        return carry

    lax.fori_loop(0, owners, send_step, 0)

    for chunk in range(width // 128):
        here = slice(chunk * 128, (chunk + 1) * 128)
        latent_t[here, :] = latent_ref[:, here].astype(F32).T.astype(BF16)
    stage[...] = jnp.zeros_like(stage)

    def turn_proj(chunk, carry):
        start = pl.multiple_of(chunk * 128, 128)
        stage[0:channels, :] = proj_ref[:, pl.ds(start, 128)].astype(F32)
        proj_t[pl.ds(start, 128), :] = stage[...].T.astype(BF16)
        return carry

    lax.fori_loop(0, 2 * width // 128, turn_proj, 0)

    chips = owners // CORES
    lane = lax.broadcasted_iota(jnp.int32, (chips, capacity), 1)
    slot_row = lax.broadcasted_iota(jnp.int32, (capacity, capacity), 0)
    slot_lane = lax.broadcasted_iota(jnp.int32, (capacity, capacity), 1)
    owner_lane = lax.broadcasted_iota(jnp.int32, (owners, owners), 1)
    own = jnp.sum(jnp.where(owner_lane == seq, count_ref[...], 0), axis=1, keepdims=True)
    counts[...] = jnp.broadcast_to(own, (owners, capacity))

    def of_core(ref, which):
        return ref[pl.ds(which, chips, stride=CORES), :]

    def picks(parity, which):
        wanted = slot_row == 2 * (slot_lane - which * half) + parity
        in_half = (slot_lane >= which * half) & (slot_lane < (which + 1) * half)
        return jnp.where(wanted & in_half, 1.0, 0.0)

    found = jnp.zeros((chips, capacity), F32)
    for which in range(CORES):
        found = found + jnp.dot(
            of_core(target_ref, which).astype(F32), picks(0, which),
            precision=lax.Precision.HIGHEST, preferred_element_type=F32,
        )
    targets[...] = found.astype(jnp.int32)
    live = jnp.where(lane < half, of_core(counts, 0), of_core(counts, 1))
    for parity in range(2):
        found = jnp.zeros((chips, capacity), F32)
        for which in range(CORES):
            found = found + jnp.dot(
                of_core(bias_ref, which), picks(parity, which),
                precision=lax.Precision.HIGHEST, preferred_element_type=F32,
            )
        biases[parity] = jnp.where(2 * (lane % half) + parity < live, found, NEG)

    reach = tables.shape[2]
    span = tables.shape[3]
    last = owners - 1

    @pl.when(seq == 0)
    def no_before():
        extended[0:reach, :] = jnp.zeros((reach, width), BF16)

    @pl.when(seq == last)
    def no_after():
        extended[reach + rows :, :] = jnp.zeros((reach, width), BF16)

    key_at = lax.broadcasted_iota(jnp.int32, (1, span), 1)
    edges = [
        jnp.where((key_at < reach) & (seq == 0), NEG, 0.0),
        jnp.where((key_at >= 2 * reach) & (seq == last), NEG, 0.0),
    ]

    def table_step(head, carry):
        row = jnp.broadcast_to(offset_ref[pl.ds(head, 1), :], (reach, span))
        spread = pltpu.roll(row, 0, 1, stride=1, stride_axis=0)
        for block in range(2):
            tables[block, head] = spread + edges[block]
        return carry

    lax.fori_loop(0, heads, table_step, 0)

    acc[...] = jnp.zeros_like(acc)
    peak_ref[...] = jnp.zeros_like(peak_ref)
    total_ref[...] = jnp.ones_like(total_ref)
    pairs = X * capacity
    low = lax.broadcasted_iota(jnp.int32, (depth, capacity), 1) < half
    peak_lane = lax.broadcasted_iota(jnp.int32, (rows, 128), 1)
    row_index = lax.broadcasted_iota(jnp.int32, (rows, pairs), 0)

    def group_step(turn, carry):
        for member_at in range(group):
            slot = turn * group + member_at

            @pl.when(slot != (Z - 1) * group + core)
            def arrive():
                pltpu.make_async_copy(
                    incoming.at[slot], incoming.at[slot], recv.at[slot]
                ).wait()

        evens, odds, rows_of, bias_of = [], [], [], [[], []]
        for shift in range(X):
            first = incoming[turn * group + CORES * shift].astype(F32)
            second = incoming[turn * group + CORES * shift + 1].astype(F32)
            evens.append(jnp.where(low, first, pltpu.roll(second, half, 1)).astype(BF16))
            odds.append(jnp.where(low, pltpu.roll(first, half, 1), second).astype(BF16))
            chip = ((x + X - shift) % X) * Z + (z + Z - z_shift(turn)) % Z
            rows_of.append(targets[pl.ds(chip, 1), :])
            for parity in range(2):
                bias_of[parity].append(biases[parity, pl.ds(chip, 1), :])
        target = jnp.concatenate(rows_of, axis=1)
        member = row_index == target
        chosen = jnp.where(member, 1.0, 0.0).astype(BF16)
        queries = jnp.dot(latent_t[...], chosen, preferred_element_type=F32)
        scores, fields = [], []
        for parity, parts in enumerate((evens, odds)):
            part = jnp.concatenate(parts, axis=1)
            keys = jnp.dot(proj_t[0:width, 0:depth], part, preferred_element_type=F32)
            logits = jnp.sum((queries * keys).reshape(heads, size, pairs), axis=1)
            scores.append(logits * (size ** -0.5) + jnp.concatenate(bias_of[parity], axis=1))
            fields.append(part)
        pair_peak = jnp.maximum(scores[0], scores[1])
        peaks = jnp.full((rows, 128), NEG, F32)
        for head in range(heads):
            column = jnp.max(
                jnp.where(member, pair_peak[head : head + 1, :], NEG), axis=1, keepdims=True
            )
            peaks = jnp.where(peak_lane == head, column, peaks)
        old = peak_ref[...]
        new = jnp.maximum(old, peaks.T[0:heads, :])
        upper = new.astype(BF16)
        lower = (new - upper.astype(F32)).astype(BF16)
        new = upper.astype(F32) + lower.astype(F32)
        peak_ref[...] = new
        factor = jnp.exp(old - new)
        slot_peak = jnp.dot(upper, chosen, preferred_element_type=F32) + jnp.dot(
            lower, chosen, preferred_element_type=F32
        )
        weights = [jnp.exp(score - slot_peak) for score in scores]
        both = weights[0] + weights[1]
        both_upper = both.astype(BF16)
        both_lower = (both - both_upper.astype(F32)).astype(BF16)
        sums = lax.dot_general(both_upper, chosen, NT, preferred_element_type=F32)
        sums = sums + lax.dot_general(both_lower, chosen, NT, preferred_element_type=F32)
        total_ref[...] = total_ref[...] * factor + sums
        mixed = None
        for parity in range(2):
            values = jnp.dot(
                proj_t[width : 2 * width, 0:depth], fields[parity], preferred_element_type=F32
            )
            term = values.reshape(heads, size, pairs) * weights[parity][:, None, :]
            mixed = term if mixed is None else mixed + term
        mixed = mixed.reshape(width, pairs).astype(BF16)
        added = lax.dot_general(mixed, chosen, NT, preferred_element_type=F32)
        acc[...] = (
            acc[...].reshape(heads, size, rows) * factor[:, None, :]
        ).reshape(width, rows) + added
        return carry

    lax.fori_loop(0, Z, group_step, 0)

    scale = 1.0 / total_ref[...]
    encoded = (acc[...].reshape(heads, size, rows) * scale[:, None, :]).reshape(width, rows)
    hidden = latent_ref[...].astype(F32) + encoded.T
    hidden_ref[...] = hidden
    center = hidden - jnp.mean(hidden, axis=1, keepdims=True)
    variance = jnp.mean(center * center, axis=1, keepdims=True)
    extended[reach : reach + rows, :] = (
        center * lax.rsqrt(variance + 1e-05) * gain_ref[...]
    ).astype(BF16)

    def halo_copy(which, there, here, to):
        return pltpu.make_async_remote_copy(
            src_ref=extended.at[there], dst_ref=extended.at[here],
            send_sem=halo_send.at[which], recv_sem=halo_recv.at[which],
            device_id=(y, to), device_id_type=MESH,
        )

    up = halo_copy(0, pl.ds(rows, reach), pl.ds(0, reach), (seq + 1) % owners)
    down = halo_copy(
        1, pl.ds(reach, reach), pl.ds(reach + rows, reach), (seq + owners - 1) % owners
    )
    pl.when(seq < last)(up.start)
    pl.when(seq > 0)(down.start)

    tile = 512
    for fetch in fetches:
        fetch.wait()

    def own_tile(index, carry):
        at = pl.ds(pl.multiple_of(index * tile, tile), tile)
        found = jnp.dot(
            extended[reach : reach + rows, :], big[:, at], preferred_element_type=F32
        )
        scaling = jnp.where(index * tile < width, size ** -0.5, 1.0)
        mixed_rows[reach : reach + rows, at] = (found * scaling).astype(BF16)
        return carry

    lax.fori_loop(0, 3 * width // tile, own_tile, 0)
    pl.when(seq > 0)(up.wait_recv)
    pl.when(seq < last)(down.wait_recv)

    def halo_tile(index, carry):
        at = pl.ds(pl.multiple_of(index * tile + width, tile), tile)
        both = jnp.concatenate([extended[0:reach, :], extended[reach + rows :, :]], axis=0)
        found = jnp.dot(both, big[:, at], preferred_element_type=F32).astype(BF16)
        mixed_rows[0:reach, at] = found[0:reach]
        mixed_rows[reach + rows :, at] = found[reach:]
        return carry

    lax.fori_loop(0, 2 * width // tile, halo_tile, 0)

    def place(y_to, x_to, z_to, core_to):
        return (y_to, x_to * (Z * CORES) + z_to * CORES + core_to)

    def remote(src_ref, dst_ref, send_sem, recv_sem, peer):
        return pltpu.make_async_remote_copy(
            src_ref=src_ref, dst_ref=dst_ref, send_sem=send_sem, recv_sem=recv_sem,
            device_id=peer, device_id_type=MESH,
        )

    part_width = width // X
    half_width = width // 2
    strip_width = half_width // Y

    def strip(who):
        return pl.ds(pl.multiple_of(half_width + who * strip_width, strip_width), strip_width)

    def part_of(turn):
        return (x + 1 + turn) % X

    def core_copy(turn):
        part = part_of(turn)
        return remote(
            grads.at[part, :, 1 - core], from_core.at[part], core_send.at[part],
            core_recv.at[part], place(y, x, z, 1 - core),
        )

    def x_copy(turn):
        part = part_of(turn)
        return remote(
            merged.at[part, :, :, pl.ds(0, half_width)], x_in.at[turn], x_send.at[turn],
            x_recv.at[turn], place(y, part, z, core),
        )

    def y_copy(turn, k):
        part = part_of(turn)
        return remote(
            merged.at[part, :, :, strip((y + k) % Y)], v_in.at[k - 1, part],
            y_send.at[k - 1, part], y_recv.at[k - 1, part], y_peers[k - 1],
        )

    def pass_part(turn, with_x):
        part = part_of(turn)
        core_copy(turn).wait_recv()
        merged[part] = (
            grads[part, :, core].astype(F32) + from_core[part].astype(F32)
        ).astype(BF16)
        for k in range(1, Y):
            y_copy(turn, k).start()
        if with_x:
            x_copy(turn).start()

    def part_step(turn, carry):
        part = part_of(turn)

        def columns(base):
            return pl.ds(pl.multiple_of(base + part * part_width, part_width), part_width)

        for block in range(2):
            mine = slice((block + 1) * reach, (block + 2) * reach)
            theirs = slice(block * reach, block * reach + span)
            queries = mixed_rows[mine, columns(0)]
            keys = mixed_rows[theirs, columns(width)]
            values = mixed_rows[theirs, columns(2 * width)]
            made = []
            for head in range(heads // X):
                here = slice(head * size, (head + 1) * size)
                logits = lax.dot_general(
                    queries[:, here], keys[:, here], NT, preferred_element_type=F32
                ) + tables[block, part * (heads // X) + head]
                powered = jnp.exp(logits - jnp.max(logits, axis=1, keepdims=True))
                total = jnp.sum(powered, axis=1, keepdims=True)
                mixture = jnp.dot(
                    powered.astype(BF16), values[:, here], preferred_element_type=F32
                )
                made.append((mixture / total).astype(BF16))
            attended[block * reach : (block + 1) * reach, columns(0)] = jnp.concatenate(
                made, axis=1
            )
        found = lax.dot_general(
            attended[:, columns(0)], cotangent[0], TN, preferred_element_type=F32
        )
        grads[part] = found.astype(BF16).reshape(Z, CORES, 16, width)
        core_copy(turn).start()

        @pl.when(turn > 0)
        def pass_earlier():
            pass_part(turn - 1, True)

        return carry

    lax.fori_loop(0, X, part_step, 0)
    pass_part(X - 1, False)

    def out_tile(index, carry):
        at = pl.ds(pl.multiple_of(index * tile, tile), tile)
        processed_ref[:, at] = (
            hidden_ref[:, at]
            + jnp.dot(attended[...], out_proj[:, at], preferred_element_type=F32)
        ).astype(BF16)
        return carry

    lax.fori_loop(0, width // tile, out_tile, 0)

    z_peers = [place(y, x, (z + k) % Z, core) for k in range(1, Z)]
    x_peers = [place(y, (x + k) % X, z, core) for k in range(1, X)]
    for turn in range(X - 1):
        x_copy(turn).wait_recv()
    x_sum[...] = (
        merged[x, :, :, 0:half_width].astype(F32)
        + (x_in[0].astype(F32) + x_in[1].astype(F32) + x_in[2].astype(F32))
    ).astype(BF16)
    z_copies = [
        remote(x_sum.at[(z + k) % Z], z_in.at[k - 1], z_send.at[k - 1], z_recv.at[k - 1], z_peers[k - 1])
        for k in range(1, Z)
    ]
    for copy in z_copies:
        copy.start()
    for turn in range(X):
        for k in range(1, Y):
            y_copy(turn, k).wait_recv()
    v_sum[...] = (
        merged[:, :, :, strip(y)].astype(F32)
        + (v_in[0].astype(F32) + v_in[1].astype(F32) + v_in[2].astype(F32))
    ).astype(BF16)
    u_copies = [
        remote(v_sum.at[(x + k) % X], u_in.at[k - 1], u_send.at[k - 1], u_recv.at[k - 1], x_peers[k - 1])
        for k in range(1, X)
    ]
    for copy in u_copies:
        copy.start()
    for copy in z_copies:
        copy.wait_recv()
    found = x_sum[z].astype(F32)
    for k in range(Z - 1):
        found = found + z_in[k].astype(F32)
    y_all[y] = found
    s_copies = [
        remote(y_all.at[y], y_all.at[y], s_send.at[k - 1], s_recv.at[k - 1], y_peers[k - 1])
        for k in range(1, Y)
    ]
    for copy in s_copies:
        copy.start()
    for copy in u_copies:
        copy.wait_recv()
    u_sum[...] = (
        v_sum[x].astype(F32)
        + (u_in[0].astype(F32) + u_in[1].astype(F32) + u_in[2].astype(F32))
    ).astype(BF16)
    w_copies = [
        remote(u_sum.at[(z + k) % Z], w_in.at[k - 1], w_send.at[k - 1], w_recv.at[k - 1], z_peers[k - 1])
        for k in range(1, Z)
    ]
    for copy in w_copies:
        copy.start()
    for copy in w_copies:
        copy.wait_recv()
    found = u_sum[z].astype(F32)
    for k in range(Z - 1):
        found = found + w_in[k].astype(F32)
    r_all[y] = found
    r_copies = [
        remote(r_all.at[y], r_all.at[y], r_send.at[k - 1], r_recv.at[k - 1], y_peers[k - 1])
        for k in range(1, Y)
    ]
    for copy in r_copies:
        copy.start()
    for copy in s_copies:
        copy.wait_recv()
    gradient_ref[:, 0:half_width] = (y_all[0] + y_all[1]) + (y_all[2] + y_all[3])
    for copy in r_copies:
        copy.wait_recv()
    for k in range(Y):
        at = half_width + k * strip_width
        gradient_ref[:, at : at + strip_width] = r_all[k]

    def sent_step(step, carry):
        to, copy = block_copy(step)

        @pl.when(to != seq)
        def done():
            copy.wait_send()

        return carry

    lax.fori_loop(0, owners, sent_step, 0)
    pl.when(seq < last)(up.wait_send)
    pl.when(seq > 0)(down.wait_send)
    for turn in range(X):
        core_copy(turn).wait_send()
        for k in range(1, Y):
            y_copy(turn, k).wait_send()
    for turn in range(X - 1):
        x_copy(turn).wait_send()
    for copy in z_copies + u_copies + s_copies + w_copies + r_copies:
        copy.wait_send()


def shards(
    grid_fields, mesh_latent, edge_source, edge_target, edge_count, edge_bias, encoder_proj,
    norm_gain, processor_proj, offset_bias, windows, output_proj, cotangent,
):
    shard_count = lax.axis_size("seq")
    device = lax.axis_index("seq")
    rows, width = mesh_latent.shape
    heads = offset_bias.shape[0]
    reach = (offset_bias.shape[1] - 1) // 2
    channels, points = grid_fields.shape[1:]
    capacity = edge_source.shape[2]
    offset = jnp.arange(3 * reach, dtype=jnp.int32) - reach
    table = jnp.where(
        jnp.abs(offset)[None, :] <= windows[:, None],
        jnp.pad(offset_bias, ((0, 0), (0, reach - 1))),
        NEG,
    )
    depth = (channels + 15) // 16 * 16
    chips = shard_count // CORES
    strip_width = width // 2 // Y
    dma = pltpu.SemaphoreType.DMA
    hbm = pl.BlockSpec(memory_space=pltpu.HBM)
    processed, gradient = pl.pallas_call(
        layer_kernel,
        out_shape=(
            jax.ShapeDtypeStruct((rows, width), BF16),
            jax.ShapeDtypeStruct((16, width), F32),
        ),
        in_specs=[pl.BlockSpec(memory_space=pltpu.SMEM)] + [vmem()] * 8 + [hbm] * 3,
        out_specs=(vmem(), vmem()),
        scratch_shapes=[
            pltpu.VMEM((points, 128), F32),
            pltpu.VMEM((128, 128), F32),
            pltpu.VMEM((shard_count, depth, capacity), BF16),
            pltpu.VMEM((shard_count, depth, capacity), BF16),
            pltpu.VMEM((width, rows), BF16),
            pltpu.VMEM((2 * width, 128), BF16),
            pltpu.VMEM((shard_count, capacity), jnp.int32),
            pltpu.VMEM((chips, capacity), jnp.int32),
            pltpu.VMEM((2, chips, capacity), F32),
            pltpu.VMEM((width, rows), F32),
            pltpu.VMEM((heads, rows), F32),
            pltpu.VMEM((heads, rows), F32),
            dma((shard_count,)),
            dma((shard_count,)),
            pltpu.VMEM((width, 3 * width), BF16),
            pltpu.VMEM((width, width), BF16),
            pltpu.VMEM((1, rows, width), BF16),
            dma((3,)),
            pltpu.VMEM((rows, width), F32),
            pltpu.VMEM((rows + 2 * reach, width), BF16),
            pltpu.VMEM((rows + 2 * reach, 3 * width), BF16),
            pltpu.VMEM((2, heads, reach, 3 * reach), F32),
            pltpu.VMEM((rows, width), BF16),
            dma((2,)),
            dma((2,)),
            pltpu.VMEM((X, Z, CORES, 16, width), BF16),
            pltpu.VMEM((X, Z, 16, width), BF16),
            pltpu.VMEM((X, Z, 16, width), BF16),
            pltpu.VMEM((X - 1, Z, 16, width // 2), BF16),
            pltpu.VMEM((Z, 16, width // 2), BF16),
            pltpu.VMEM((Z - 1, 16, width // 2), BF16),
            pltpu.VMEM((Y, 16, width // 2), F32),
            pltpu.VMEM((Y - 1, X, Z, 16, strip_width), BF16),
            pltpu.VMEM((X, Z, 16, strip_width), BF16),
            pltpu.VMEM((X - 1, Z, 16, strip_width), BF16),
            pltpu.VMEM((Z, 16, strip_width), BF16),
            pltpu.VMEM((Z - 1, 16, strip_width), BF16),
            pltpu.VMEM((Y, 16, strip_width), F32),
            dma((X,)),
            dma((X,)),
            dma((X - 1,)),
            dma((X - 1,)),
            dma((Y - 1, X)),
            dma((Y - 1, X)),
            dma((Z - 1,)),
            dma((Z - 1,)),
            dma((Y - 1,)),
            dma((Y - 1,)),
            dma((X - 1,)),
            dma((X - 1,)),
            dma((Z - 1,)),
            dma((Z - 1,)),
            dma((Y - 1,)),
            dma((Y - 1,)),
        ],
        compiler_params=pltpu.CompilerParams(
            vmem_limit_bytes=VMEM_LIMIT, collective_id=2, has_side_effects=True
        ),
        name="layer",
    )(
        edge_source[0], grid_fields, edge_target[0], edge_count, edge_bias[0], mesh_latent,
        encoder_proj, norm_gain[None], table, processor_proj, output_proj, cotangent,
    )

    return (processed[None], gradient)


def solution(mesh):
    in_specs = (
        P("dp", None, "seq"),
        P("seq", None),
        P("seq", None, None),
        P("seq", None, None),
        P(),
        P("seq", None, None),
        P(),
        P(),
        P(),
        P(),
        P(),
        P(),
        P("dp", "seq", None),
    )
    out_specs = (P("dp", "seq", None), P("seq", None))
    return jax.shard_map(shards, mesh=mesh, in_specs=in_specs, out_specs=out_specs, check_vma=False)
```

time: 141 us -> 115 us (0.82)
  Pallas kernels: 126 us -> 109 us
  waiting for transfers between devices: 4.87 us -> 0 us
  starting transfers between devices: 4.68 us -> 0 us
    pallas_call x3 -> x1, Pallas kernels: 126 us -> 109 us  [shards(): pl.pallas_call(layer_kernel, out_shape=(jax.ShapeDtypeStruct((rows, width...]
    ppermute x2 -> x0, waiting for transfers between devices: 4.87 us -> none  [the longest x1 3.82 us: shards(): before = lax.ppermute(normalized[rows - reach:], 'seq', up)]
    ppermute x2 -> x0, starting transfers between devices: 4.68 us -> none  [the longest x1 2.58 us: shards(): after = lax.ppermute(normalized[:reach], 'seq', down)]
    unnamed x9 -> x2, local copies, waits for them, and re-layouts: 2.17 us -> 3.34 us
  transfers between devices with their start and end apart: 2 -> 0, of which waited for: 2 -> 0; matrix products, arithmetic and copies ran while one was open for 0% -> 0% of each run, Pallas kernels for 0% -> 0%
where the time goes in v3:
time: 115 us; the launch traced here: 114 us
  Pallas kernels  109 us (95%)
  local copies, waits for them, and re-layouts  3.34 us (3%)
  other arithmetic  1.43 us (1%)
    pallas_call x1, Pallas kernels, shards(): pl.pallas_call(layer_kernel, out_shape=(jax.ShapeDtypeStruct((rows, width...  109 us
    unnamed x2, local copies, waits for them, and re-layouts  3.34 us

profile of v3, /device:TPU:32, one launch (start us, length us, event | category | flops | bytes accessed | tf_op | source)
XLA Modules:
  0.0 114.5 jit_solution(6919558792916977705)
XLA Ops:
  0.6 1.4 %pad_select_fusion.offset_ref = f32[16,384]{1,0:T(8,128)} fusion(f32[16,257]{1,0:T(8,128)} %param.22, s32[384]{0:T(512)S(1)} %add_abs_fusion, s32[16]{0:T(128)} %param.23), kind=kLoop, calls=%fused_computation | loop fusion | flops 12288 | bytes 42624 | tf_op jit(solution)/shard_map/jit(_where)/select_n | solution.py:524
  2.1 109.1 %layer.1 = (bf16[256,1024]{1,0:T(8,128)(2,1)}, f32[16,1024]{1,0:T(8,128)}) custom-call(s32[64,128]{1,0:T(8,128)} %bitcast.6, bf16[1,100,4096]{2,1,0:T(8,128)(2,1)} %grid_ref.1, s32[64,128]{1,0:T(8,128)} %bitcast.7, s32[64,64]{1,0:T(8,128)} %count_ref.1, f32[64,128]{1,0:T(8,128)} %bitcast.8, bf16[256,1024]{1,0:T(8,128)(2,1)} %latent_ref.1, ...), custom_call_target="tpu_custom_call" | custom-call | tf_op jit(solution)/shard_map/layer/pallas_call | solution.py:534
  111.2 1.9 %copy.17 = bf16[1,256,1024]{2,1,0:T(8,128)(2,1)} copy(bf16[1,256,1024]{2,1,0:T(8,128)(2,1)} %bitcast.5) | data formatting | bytes 1048576
  113.0 1.5 %copy.18 = f32[16,1024]{1,0:T(8,128)} copy(f32[16,1024]{1,0:T(8,128)} %get-tuple-element.9) | data formatting | bytes 131072
  (1 shorter events, 0.0 us)

commit v4 on v3

--- a/solution.py
+++ b/solution.py
@@ -7,6 +7,7 @@
 
 MESH = pl.DeviceIdType.MESH
 X, Z, CORES, Y = 4, 8, 2, 4
+UNITS = 4
 NEG = -1e30
 F32 = jnp.float32
 BF16 = jnp.bfloat16
@@ -21,14 +22,13 @@
 
 
 def layer_kernel(
-    source_ref, grid_ref, target_ref, count_ref, bias_ref, latent_ref, proj_ref, gain_ref,
-    offset_ref, big_hbm, out_hbm, cotangent_hbm,
+    source_ref, windows_ref, grid_ref, target_ref, count_ref, bias_ref, latent_ref, proj_ref,
+    gain_ref, offset_ref, big_hbm, out_hbm, cotangent_hbm,
     processed_ref, gradient_ref, table, stage, outgoing, incoming, latent_t, proj_t, counts,
     targets, biases, acc, peak_ref, total_ref, send, recv,
-    big, out_proj, cotangent, fetched, hidden_ref, extended, mixed_rows, tables, attended,
-    halo_send, halo_recv, grads, from_core, merged, x_in, x_sum, z_in, y_all, v_in, v_sum,
-    u_in, u_sum, w_in, r_all, core_send, core_recv, x_send, x_recv, y_send, y_recv, z_send,
-    z_recv, s_send, s_recv, u_send, u_recv, w_send, w_recv, r_send, r_recv,
+    big, out_proj, cotangent, fetched, hidden_ref, extended, mixed_rows, offsets, tables,
+    attended_t, attended, halo_send, halo_recv, grads, from_core, merged, v_in, v_sum, w_in,
+    r_all, core_send, core_recv, y_send, y_recv, w_send, w_recv, r_send, r_recv,
 ):
     seq = lax.axis_index("seq")
     y = lax.axis_index("dp")
@@ -41,11 +41,15 @@
     heads = peak_ref.shape[0]
     size = width // heads
     half = capacity // 2
-    group = 2 * X
+    group = CORES * UNITS
     depth = outgoing.shape[1]
 
-    def z_shift(turn):
-        return 4 + (1 - 2 * (turn % 2)) * ((turn + 1) // 2)
+    def shifts(turn, chip_at):
+        pair_at, unit = turn * (UNITS // 2) + chip_at // 2, chip_at % 2
+        lap, leg = pair_at // 4, pair_at % 4
+        x_shift = 2 + (1 - 2 * (lap % 2)) * ((lap + 1) // 2)
+        z_shift = (1 - unit) * (4 - leg) + unit * (leg + 4 * ((leg + 3) // 4))
+        return x_shift, z_shift
 
     barrier = pltpu.get_barrier_semaphore()
 
@@ -78,8 +82,9 @@
     pl.semaphore_wait(barrier, owners - 1 + Y - 1)
 
     def block_copy(step):
-        to_x = (x + (step // CORES) % X) % X
-        to_z = (z + z_shift(step // group)) % Z
+        x_shift, z_shift = shifts(step // group, (step // CORES) % UNITS)
+        to_x = (x + x_shift) % X
+        to_z = (z + z_shift) % Z
         to = to_x * (Z * CORES) + to_z * CORES + step % CORES
         slot = step - step % CORES + core
         copy = pltpu.make_async_remote_copy(
@@ -155,8 +160,7 @@
             )
         biases[parity] = jnp.where(2 * (lane % half) + parity < live, found, NEG)
 
-    reach = tables.shape[2]
-    span = tables.shape[3]
+    span, reach = tables.shape[2], tables.shape[3] // 2
     last = owners - 1
 
     @pl.when(seq == 0)
@@ -167,25 +171,33 @@
     def no_after():
         extended[reach + rows :, :] = jnp.zeros((reach, width), BF16)
 
-    key_at = lax.broadcasted_iota(jnp.int32, (1, span), 1)
+    offsets[...] = jnp.zeros_like(offsets)
+    offsets[:, 0 : 2 * reach + 1] = offset_ref[...]
+    key_lane = lax.broadcasted_iota(jnp.int32, (1, span), 1)
+    key_row = lax.broadcasted_iota(jnp.int32, (span, reach), 0)
     edges = [
-        jnp.where((key_at < reach) & (seq == 0), NEG, 0.0),
-        jnp.where((key_at >= 2 * reach) & (seq == last), NEG, 0.0),
+        jnp.where((key_row < reach) & (seq == 0), NEG, 0.0),
+        jnp.where((key_row >= 2 * reach) & (seq == last), NEG, 0.0),
     ]
 
-    def table_step(head, carry):
-        row = jnp.broadcast_to(offset_ref[pl.ds(head, 1), :], (reach, span))
-        spread = pltpu.roll(row, 0, 1, stride=1, stride_axis=0)
-        for block in range(2):
-            tables[block, head] = spread + edges[block]
-        return carry
-
-    lax.fori_loop(0, heads, table_step, 0)
+    def table_step(pair, carry):
+        for side in range(2):
+            head = pair * 2 + side
+            row = jnp.where(
+                jnp.abs(key_lane - reach) <= windows_ref[head], offsets[pl.ds(head, 1), :], NEG
+            )
+            row = jnp.broadcast_to(row, (reach, span))
+            spread = pltpu.roll(row, 0, 1, stride=1, stride_axis=0).T
+            for block in range(2):
+                tables[block, pair, :, side * reach : (side + 1) * reach] = spread + edges[block]
+        return carry
+
+    lax.fori_loop(0, heads // 2, table_step, 0)
 
     acc[...] = jnp.zeros_like(acc)
     peak_ref[...] = jnp.zeros_like(peak_ref)
     total_ref[...] = jnp.ones_like(total_ref)
-    pairs = X * capacity
+    pairs = UNITS * capacity
     low = lax.broadcasted_iota(jnp.int32, (depth, capacity), 1) < half
     peak_lane = lax.broadcasted_iota(jnp.int32, (rows, 128), 1)
     row_index = lax.broadcasted_iota(jnp.int32, (rows, pairs), 0)
@@ -194,19 +206,20 @@
         for member_at in range(group):
             slot = turn * group + member_at
 
-            @pl.when(slot != (Z - 1) * group + core)
+            @pl.when(slot != 25 * CORES + core)
             def arrive():
                 pltpu.make_async_copy(
                     incoming.at[slot], incoming.at[slot], recv.at[slot]
                 ).wait()
 
         evens, odds, rows_of, bias_of = [], [], [], [[], []]
-        for shift in range(X):
-            first = incoming[turn * group + CORES * shift].astype(F32)
-            second = incoming[turn * group + CORES * shift + 1].astype(F32)
+        for unit in range(UNITS):
+            first = incoming[turn * group + CORES * unit].astype(F32)
+            second = incoming[turn * group + CORES * unit + 1].astype(F32)
             evens.append(jnp.where(low, first, pltpu.roll(second, half, 1)).astype(BF16))
             odds.append(jnp.where(low, pltpu.roll(first, half, 1), second).astype(BF16))
-            chip = ((x + X - shift) % X) * Z + (z + Z - z_shift(turn)) % Z
+            x_shift, z_shift = shifts(turn, unit)
+            chip = ((x + X - x_shift) % X) * Z + (z + Z - z_shift) % Z
             rows_of.append(targets[pl.ds(chip, 1), :])
             for parity in range(2):
                 bias_of[parity].append(biases[parity, pl.ds(chip, 1), :])
@@ -259,7 +272,7 @@
         ).reshape(width, rows) + added
         return carry
 
-    lax.fori_loop(0, Z, group_step, 0)
+    lax.fori_loop(0, owners // group, group_step, 0)
 
     scale = 1.0 / total_ref[...]
     encoded = (acc[...].reshape(heads, size, rows) * scale[:, None, :]).reshape(width, rows)
@@ -322,11 +335,10 @@
         )
 
     part_width = width // X
-    half_width = width // 2
-    strip_width = half_width // Y
+    strip_width = width // Y
 
     def strip(who):
-        return pl.ds(pl.multiple_of(half_width + who * strip_width, strip_width), strip_width)
+        return pl.ds(pl.multiple_of(who * strip_width, strip_width), strip_width)
 
     def part_of(turn):
         return (x + 1 + turn) % X
@@ -338,13 +350,6 @@
             core_recv.at[part], place(y, x, z, 1 - core),
         )
 
-    def x_copy(turn):
-        part = part_of(turn)
-        return remote(
-            merged.at[part, :, :, pl.ds(0, half_width)], x_in.at[turn], x_send.at[turn],
-            x_recv.at[turn], place(y, part, z, core),
-        )
-
     def y_copy(turn, k):
         part = part_of(turn)
         return remote(
@@ -352,7 +357,15 @@
             y_send.at[k - 1, part], y_recv.at[k - 1, part], y_peers[k - 1],
         )
 
-    def pass_part(turn, with_x):
+    def w_copy(turn, k):
+        part = part_of(turn)
+        to_z = (z + k) % Z
+        return remote(
+            v_sum.at[part, to_z], w_in.at[turn, k], w_send.at[turn, k], w_recv.at[turn, k],
+            place(y, part, to_z, core),
+        )
+
+    def pass_to_y(turn):
         part = part_of(turn)
         core_copy(turn).wait_recv()
         merged[part] = (
@@ -360,132 +373,98 @@
         ).astype(BF16)
         for k in range(1, Y):
             y_copy(turn, k).start()
-        if with_x:
-            x_copy(turn).start()
+
+    def pass_to_owners(turn, first):
+        part = part_of(turn)
+        for k in range(1, Y):
+            y_copy(turn, k).wait_recv()
+        v_sum[part] = (
+            merged[part, :, :, strip(y)].astype(F32)
+            + (v_in[0, part].astype(F32) + v_in[1, part].astype(F32) + v_in[2, part].astype(F32))
+        ).astype(BF16)
+        for k in range(first, Z):
+            w_copy(turn, k).start()
+
+    side_lane = lax.broadcasted_iota(jnp.int32, (reach, 2 * size), 1) < size
 
     def part_step(turn, carry):
         part = part_of(turn)
 
-        def columns(base):
-            return pl.ds(pl.multiple_of(base + part * part_width, part_width), part_width)
-
+        def columns(base, pair):
+            at = base + part * part_width + pair * 2 * size
+            return pl.ds(pl.multiple_of(at, 2 * size), 2 * size)
+
+        pairs_in_part = part_width // (2 * size)
         for block in range(2):
             mine = slice((block + 1) * reach, (block + 2) * reach)
             theirs = slice(block * reach, block * reach + span)
-            queries = mixed_rows[mine, columns(0)]
-            keys = mixed_rows[theirs, columns(width)]
-            values = mixed_rows[theirs, columns(2 * width)]
-            made = []
-            for head in range(heads // X):
-                here = slice(head * size, (head + 1) * size)
+            for pair in range(pairs_in_part):
+                queries = mixed_rows[mine, columns(0, pair)]
+                none = jnp.zeros_like(queries)
+                queries = jnp.concatenate(
+                    [jnp.where(side_lane, queries, none), jnp.where(side_lane, none, queries)],
+                    axis=0,
+                )
                 logits = lax.dot_general(
-                    queries[:, here], keys[:, here], NT, preferred_element_type=F32
-                ) + tables[block, part * (heads // X) + head]
-                powered = jnp.exp(logits - jnp.max(logits, axis=1, keepdims=True))
-                total = jnp.sum(powered, axis=1, keepdims=True)
-                mixture = jnp.dot(
-                    powered.astype(BF16), values[:, here], preferred_element_type=F32
-                )
-                made.append((mixture / total).astype(BF16))
-            attended[block * reach : (block + 1) * reach, columns(0)] = jnp.concatenate(
-                made, axis=1
-            )
-        found = lax.dot_general(
-            attended[:, columns(0)], cotangent[0], TN, preferred_element_type=F32
+                    mixed_rows[theirs, columns(width, pair)], queries, NT,
+                    preferred_element_type=F32,
+                ) + tables[block, part * pairs_in_part + pair]
+                powered = jnp.exp(logits - jnp.max(logits, axis=0, keepdims=True))
+                scale = 1.0 / jnp.sum(powered, axis=0, keepdims=True)
+                mixture = lax.dot_general(
+                    mixed_rows[theirs, columns(2 * width, pair)], powered.astype(BF16), TN,
+                    preferred_element_type=F32,
+                ) * scale
+                across = slice(block * reach, (block + 1) * reach)
+                for side in range(2):
+                    down_at = part * part_width + (pair * 2 + side) * size
+                    attended_t[pl.ds(pl.multiple_of(down_at, size), size), across] = mixture[
+                        side * size : (side + 1) * size, side * reach : (side + 1) * reach
+                    ].astype(BF16)
+        found = jnp.dot(
+            attended_t[pl.ds(pl.multiple_of(part * part_width, part_width), part_width), :],
+            cotangent[0], preferred_element_type=F32,
         )
         grads[part] = found.astype(BF16).reshape(Z, CORES, 16, width)
         core_copy(turn).start()
 
         @pl.when(turn > 0)
-        def pass_earlier():
-            pass_part(turn - 1, True)
+        def pass_one():
+            pass_to_y(turn - 1)
+
+        @pl.when(turn > 1)
+        def pass_two():
+            pass_to_owners(turn - 2, 0)
 
         return carry
 
     lax.fori_loop(0, X, part_step, 0)
-    pass_part(X - 1, False)
-
-    def out_tile(index, carry):
-        at = pl.ds(pl.multiple_of(index * tile, tile), tile)
+    pass_to_owners(X - 2, 0)
+    attended[...] = attended_t[...].astype(F32).T.astype(BF16)
+
+    def out_tile(index):
+        at = slice(index * tile, (index + 1) * tile)
         processed_ref[:, at] = (
             hidden_ref[:, at]
             + jnp.dot(attended[...], out_proj[:, at], preferred_element_type=F32)
         ).astype(BF16)
-        return carry
-
-    lax.fori_loop(0, width // tile, out_tile, 0)
-
-    z_peers = [place(y, x, (z + k) % Z, core) for k in range(1, Z)]
-    x_peers = [place(y, (x + k) % X, z, core) for k in range(1, X)]
-    for turn in range(X - 1):
-        x_copy(turn).wait_recv()
-    x_sum[...] = (
-        merged[x, :, :, 0:half_width].astype(F32)
-        + (x_in[0].astype(F32) + x_in[1].astype(F32) + x_in[2].astype(F32))
-    ).astype(BF16)
-    z_copies = [
-        remote(x_sum.at[(z + k) % Z], z_in.at[k - 1], z_send.at[k - 1], z_recv.at[k - 1], z_peers[k - 1])
-        for k in range(1, Z)
-    ]
-    for copy in z_copies:
-        copy.start()
+
+    pass_to_y(X - 1)
+    for index in range(width // tile):
+        out_tile(index)
+    pass_to_owners(X - 1, 1)
+    total = v_sum[x, z].astype(F32)
     for turn in range(X):
-        for k in range(1, Y):
-            y_copy(turn, k).wait_recv()
-    v_sum[...] = (
-        merged[:, :, :, strip(y)].astype(F32)
-        + (v_in[0].astype(F32) + v_in[1].astype(F32) + v_in[2].astype(F32))
-    ).astype(BF16)
-    u_copies = [
-        remote(v_sum.at[(x + k) % X], u_in.at[k - 1], u_send.at[k - 1], u_recv.at[k - 1], x_peers[k - 1])
-        for k in range(1, X)
-    ]
-    for copy in u_copies:
-        copy.start()
-    for copy in z_copies:
-        copy.wait_recv()
-    found = x_sum[z].astype(F32)
-    for k in range(Z - 1):
-        found = found + z_in[k].astype(F32)
-    y_all[y] = found
-    s_copies = [
-        remote(y_all.at[y], y_all.at[y], s_send.at[k - 1], s_recv.at[k - 1], y_peers[k - 1])
-        for k in range(1, Y)
-    ]
-    for copy in s_copies:
-        copy.start()
-    for copy in u_copies:
-        copy.wait_recv()
-    u_sum[...] = (
-        v_sum[x].astype(F32)
-        + (u_in[0].astype(F32) + u_in[1].astype(F32) + u_in[2].astype(F32))
-    ).astype(BF16)
-    w_copies = [
-        remote(u_sum.at[(z + k) % Z], w_in.at[k - 1], w_send.at[k - 1], w_recv.at[k - 1], z_peers[k - 1])
-        for k in range(1, Z)
-    ]
-    for copy in w_copies:
-        copy.start()
-    for copy in w_copies:
-        copy.wait_recv()
-    found = u_sum[z].astype(F32)
-    for k in range(Z - 1):
-        found = found + w_in[k].astype(F32)
-    r_all[y] = found
+        for k in range(1 if turn == X - 1 else 0, Z):
+            w_copy(turn, k).wait_recv()
+            total = total + w_in[turn, k].astype(F32)
+    r_all[y] = total
     r_copies = [
         remote(r_all.at[y], r_all.at[y], r_send.at[k - 1], r_recv.at[k - 1], y_peers[k - 1])
         for k in range(1, Y)
     ]
     for copy in r_copies:
         copy.start()
-    for copy in s_copies:
-        copy.wait_recv()
-    gradient_ref[:, 0:half_width] = (y_all[0] + y_all[1]) + (y_all[2] + y_all[3])
-    for copy in r_copies:
-        copy.wait_recv()
-    for k in range(Y):
-        at = half_width + k * strip_width
-        gradient_ref[:, at : at + strip_width] = r_all[k]
 
     def sent_step(step, carry):
         to, copy = block_copy(step)
@@ -503,9 +482,13 @@
         core_copy(turn).wait_send()
         for k in range(1, Y):
             y_copy(turn, k).wait_send()
-    for turn in range(X - 1):
-        x_copy(turn).wait_send()
-    for copy in z_copies + u_copies + s_copies + w_copies + r_copies:
+        for k in range(1 if turn == X - 1 else 0, Z):
+            w_copy(turn, k).wait_send()
+    for copy in r_copies:
+        copy.wait_recv()
+    for k in range(Y):
+        gradient_ref[:, k * strip_width : (k + 1) * strip_width] = r_all[k]
+    for copy in r_copies:
         copy.wait_send()
 
 
@@ -520,15 +503,9 @@
     reach = (offset_bias.shape[1] - 1) // 2
     channels, points = grid_fields.shape[1:]
     capacity = edge_source.shape[2]
-    offset = jnp.arange(3 * reach, dtype=jnp.int32) - reach
-    table = jnp.where(
-        jnp.abs(offset)[None, :] <= windows[:, None],
-        jnp.pad(offset_bias, ((0, 0), (0, reach - 1))),
-        NEG,
-    )
     depth = (channels + 15) // 16 * 16
     chips = shard_count // CORES
-    strip_width = width // 2 // Y
+    strip_width = width // Y
     dma = pltpu.SemaphoreType.DMA
     hbm = pl.BlockSpec(memory_space=pltpu.HBM)
     processed, gradient = pl.pallas_call(
@@ -537,7 +514,7 @@
             jax.ShapeDtypeStruct((rows, width), BF16),
             jax.ShapeDtypeStruct((16, width), F32),
         ),
-        in_specs=[pl.BlockSpec(memory_space=pltpu.SMEM)] + [vmem()] * 8 + [hbm] * 3,
+        in_specs=[pl.BlockSpec(memory_space=pltpu.SMEM)] * 2 + [vmem()] * 8 + [hbm] * 3,
         out_specs=(vmem(), vmem()),
         scratch_shapes=[
             pltpu.VMEM((points, 128), F32),
@@ -561,37 +538,25 @@
             pltpu.VMEM((rows, width), F32),
             pltpu.VMEM((rows + 2 * reach, width), BF16),
             pltpu.VMEM((rows + 2 * reach, 3 * width), BF16),
-            pltpu.VMEM((2, heads, reach, 3 * reach), F32),
+            pltpu.VMEM((heads, 3 * reach), F32),
+            pltpu.VMEM((2, heads // 2, 3 * reach, 2 * reach), F32),
+            pltpu.VMEM((width, rows), BF16),
             pltpu.VMEM((rows, width), BF16),
             dma((2,)),
             dma((2,)),
             pltpu.VMEM((X, Z, CORES, 16, width), BF16),
             pltpu.VMEM((X, Z, 16, width), BF16),
             pltpu.VMEM((X, Z, 16, width), BF16),
-            pltpu.VMEM((X - 1, Z, 16, width // 2), BF16),
-            pltpu.VMEM((Z, 16, width // 2), BF16),
-            pltpu.VMEM((Z - 1, 16, width // 2), BF16),
-            pltpu.VMEM((Y, 16, width // 2), F32),
             pltpu.VMEM((Y - 1, X, Z, 16, strip_width), BF16),
             pltpu.VMEM((X, Z, 16, strip_width), BF16),
-            pltpu.VMEM((X - 1, Z, 16, strip_width), BF16),
-            pltpu.VMEM((Z, 16, strip_width), BF16),
-            pltpu.VMEM((Z - 1, 16, strip_width), BF16),
+            pltpu.VMEM((X, Z, 16, strip_width), BF16),
             pltpu.VMEM((Y, 16, strip_width), F32),
             dma((X,)),
             dma((X,)),
-            dma((X - 1,)),
-            dma((X - 1,)),
             dma((Y - 1, X)),
             dma((Y - 1, X)),
-            dma((Z - 1,)),
-            dma((Z - 1,)),
-            dma((Y - 1,)),
-            dma((Y - 1,)),
-            dma((X - 1,)),
-            dma((X - 1,)),
-            dma((Z - 1,)),
-            dma((Z - 1,)),
+            dma((X, Z)),
+            dma((X, Z)),
             dma((Y - 1,)),
             dma((Y - 1,)),
         ],
@@ -600,8 +565,8 @@
         ),
         name="layer",
     )(
-        edge_source[0], grid_fields, edge_target[0], edge_count, edge_bias[0], mesh_latent,
-        encoder_proj, norm_gain[None], table, processor_proj, output_proj, cotangent,
+        edge_source[0], windows, grid_fields, edge_target[0], edge_count, edge_bias[0], mesh_latent,
+        encoder_proj, norm_gain[None], offset_bias, processor_proj, output_proj, cotangent,
     )
 
     return (processed[None], gradient)

time: 115 us -> 105 us (0.913)
  Pallas kernels: 109 us -> 101 us
  other arithmetic: 1.43 us -> 0 us
    pallas_call x1, Pallas kernels: 109 us -> 101 us  [shards(): pl.pallas_call(layer_kernel, out_shape=(jax.ShapeDtypeStruct((rows, width...]
    select_n x1 -> x0, other arithmetic: 1.42 us -> none  [shards(): jnp.where(jnp.abs(offset)[None, :] <= windows[:, None], jnp.pad(offset_bi...]
where the time goes in v4:
time: 105 us
  Pallas kernels  101 us (96%)
  local copies, waits for them, and re-layouts  3.34 us (3%)
    pallas_call x1, Pallas kernels, shards(): pl.pallas_call(layer_kernel, out_shape=(jax.ShapeDtypeStruct((rows, width...  101 us
    unnamed x2, local copies, waits for them, and re-layouts  3.34 us

profile of v4, /device:TPU:32, one launch (start us, length us, event | category | flops | bytes accessed | tf_op | source)
XLA Modules:
  0.0 105.0 jit_solution(9780252887708582514)
XLA Ops:
  0.6 101.0 %layer.1 = (bf16[256,1024]{1,0:T(8,128)(2,1)}, f32[16,1024]{1,0:T(8,128)}) custom-call(s32[64,128]{1,0:T(8,128)} %bitcast.6, s32[16]{0:T(128)} %windows_ref.1, bf16[1,100,4096]{2,1,0:T(8,128)(2,1)} %grid_ref.1, s32[64,128]{1,0:T(8,128)} %bitcast.7, s32[64,64]{1,0:T(8,128)} %count_ref.1, f32[64,128]{1,0:T(8,128)} %bitcast.8, bf16[256,1024]{1,0:T(8,128)(2,1)} %latent_ref.1, ...), custom_call_target="tpu_custom_call" | custom-call | tf_op jit(solution)/shard_map/layer/pallas_call | solution.py:511
  101.7 1.9 %copy.17 = bf16[1,256,1024]{2,1,0:T(8,128)(2,1)} copy(bf16[1,256,1024]{2,1,0:T(8,128)(2,1)} %bitcast.5) | data formatting | bytes 1048576
  103.5 1.5 %copy.18 = f32[16,1024]{1,0:T(8,128)} copy(f32[16,1024]{1,0:T(8,128)} %get-tuple-element.9) | data formatting | bytes 131072

commit v5 on v4

--- a/solution.py
+++ b/solution.py
@@ -24,8 +24,8 @@
 def layer_kernel(
     source_ref, windows_ref, grid_ref, target_ref, count_ref, bias_ref, latent_ref, proj_ref,
     gain_ref, offset_ref, big_hbm, out_hbm, cotangent_hbm,
-    processed_ref, gradient_ref, table, stage, outgoing, incoming, latent_t, proj_t, counts,
-    targets, biases, acc, peak_ref, total_ref, send, recv,
+    processed_ref, gradient_ref, table, stage, outgoing, incoming, rest_out, rest_in, latent_t, proj_t, counts,
+    targets, biases, acc, peak_ref, total_ref, send, recv, rest_send, rest_recv,
     big, out_proj, cotangent, fetched, hidden_ref, extended, mixed_rows, offsets, tables,
     attended_t, attended, halo_send, halo_recv, grads, from_core, merged, v_in, v_sum, w_in,
     r_all, core_send, core_recv, y_send, y_recv, w_send, w_recv, r_send, r_recv,
@@ -42,7 +42,8 @@
     size = width // heads
     half = capacity // 2
     group = CORES * UNITS
-    depth = outgoing.shape[1]
+    main, rest = outgoing.shape[1], rest_out.shape[1]
+    depth = main + 16
 
     def shifts(turn, chip_at):
         pair_at, unit = turn * (UNITS // 2) + chip_at // 2, chip_at % 2
@@ -92,23 +93,33 @@
             send_sem=send.at[step], recv_sem=recv.at[slot],
             device_id=(y, to), device_id_type=MESH,
         )
-        return to, copy
+        rest_copy = pltpu.make_async_remote_copy(
+            src_ref=rest_out.at[step], dst_ref=rest_in.at[slot],
+            send_sem=rest_send.at[step], recv_sem=rest_recv.at[slot],
+            device_id=(y, to), device_id_type=MESH,
+        )
+        return to, copy, rest_copy
 
     def send_step(step, carry):
-        to, copy = block_copy(step)
+        to, copy, rest_copy = block_copy(step)
         for slot in range(capacity):
             row = (slot % 2) * half + slot // 2
             stage[row : row + 1, :] = table[pl.ds(source_ref[to, slot], 1), :]
-        block = stage[...].T[0:depth, :].astype(BF16)
+        turned = stage[...].T
+        block = turned[0:main, :].astype(BF16)
+        left = turned[main : main + rest, :]
 
         @pl.when(to == seq)
         def keep():
             incoming[step] = block
+            rest_in[step] = left
 
         @pl.when(to != seq)
         def pass_on():
             outgoing[step] = block
+            rest_out[step] = left
             copy.start()
+            rest_copy.start()
 
         return carry
 
@@ -211,11 +222,18 @@
                 pltpu.make_async_copy(
                     incoming.at[slot], incoming.at[slot], recv.at[slot]
                 ).wait()
+                pltpu.make_async_copy(
+                    rest_in.at[slot], rest_in.at[slot], rest_recv.at[slot]
+                ).wait()
+
+        def arrived(slot):
+            blank = jnp.zeros((depth - main - rest, capacity), F32)
+            return jnp.concatenate([incoming[slot].astype(F32), rest_in[slot], blank], axis=0)
 
         evens, odds, rows_of, bias_of = [], [], [], [[], []]
         for unit in range(UNITS):
-            first = incoming[turn * group + CORES * unit].astype(F32)
-            second = incoming[turn * group + CORES * unit + 1].astype(F32)
+            first = arrived(turn * group + CORES * unit)
+            second = arrived(turn * group + CORES * unit + 1)
             evens.append(jnp.where(low, first, pltpu.roll(second, half, 1)).astype(BF16))
             odds.append(jnp.where(low, pltpu.roll(first, half, 1), second).astype(BF16))
             x_shift, z_shift = shifts(turn, unit)
@@ -396,6 +414,8 @@
 
         pairs_in_part = part_width // (2 * size)
         for block in range(2):
+            if block == 1:
+                pl.when(turn > 0)(lambda: pass_to_y(turn - 1))
             mine = slice((block + 1) * reach, (block + 2) * reach)
             theirs = slice(block * reach, block * reach + span)
             for pair in range(pairs_in_part):
@@ -427,19 +447,10 @@
         )
         grads[part] = found.astype(BF16).reshape(Z, CORES, 16, width)
         core_copy(turn).start()
-
-        @pl.when(turn > 0)
-        def pass_one():
-            pass_to_y(turn - 1)
-
-        @pl.when(turn > 1)
-        def pass_two():
-            pass_to_owners(turn - 2, 0)
-
         return carry
 
     lax.fori_loop(0, X, part_step, 0)
-    pass_to_owners(X - 2, 0)
+    pass_to_owners(0, 0)
     attended[...] = attended_t[...].astype(F32).T.astype(BF16)
 
     def out_tile(index):
@@ -450,8 +461,9 @@
         ).astype(BF16)
 
     pass_to_y(X - 1)
-    for index in range(width // tile):
-        out_tile(index)
+    for turn in range(1, X - 1):
+        pass_to_owners(turn, 0)
+        out_tile(turn - 1)
     pass_to_owners(X - 1, 1)
     total = v_sum[x, z].astype(F32)
     for turn in range(X):
@@ -467,11 +479,12 @@
         copy.start()
 
     def sent_step(step, carry):
-        to, copy = block_copy(step)
+        to, copy, rest_copy = block_copy(step)
 
         @pl.when(to != seq)
         def done():
             copy.wait_send()
+            rest_copy.wait_send()
 
         return carry
 
@@ -492,6 +505,11 @@
         copy.wait_send()
 
 
+def place_kernel(processed_ref, gradient_ref, processed_out, gradient_out):
+    processed_out[0] = processed_ref[...]
+    gradient_out[...] = gradient_ref[...]
+
+
 def shards(
     grid_fields, mesh_latent, edge_source, edge_target, edge_count, edge_bias, encoder_proj,
     norm_gain, processor_proj, offset_bias, windows, output_proj, cotangent,
@@ -503,7 +521,7 @@
     reach = (offset_bias.shape[1] - 1) // 2
     channels, points = grid_fields.shape[1:]
     capacity = edge_source.shape[2]
-    depth = (channels + 15) // 16 * 16
+    main = channels // 16 * 16
     chips = shard_count // CORES
     strip_width = width // Y
     dma = pltpu.SemaphoreType.DMA
@@ -519,8 +537,10 @@
         scratch_shapes=[
             pltpu.VMEM((points, 128), F32),
             pltpu.VMEM((128, 128), F32),
-            pltpu.VMEM((shard_count, depth, capacity), BF16),
-            pltpu.VMEM((shard_count, depth, capacity), BF16),
+            pltpu.VMEM((shard_count, main, capacity), BF16),
+            pltpu.VMEM((shard_count, main, capacity), BF16),
+            pltpu.VMEM((shard_count, channels - main, capacity), F32),
+            pltpu.VMEM((shard_count, channels - main, capacity), F32),
             pltpu.VMEM((width, rows), BF16),
             pltpu.VMEM((2 * width, 128), BF16),
             pltpu.VMEM((shard_count, capacity), jnp.int32),
@@ -529,6 +549,8 @@
             pltpu.VMEM((width, rows), F32),
             pltpu.VMEM((heads, rows), F32),
             pltpu.VMEM((heads, rows), F32),
+            dma((shard_count,)),
+            dma((shard_count,)),
             dma((shard_count,)),
             dma((shard_count,)),
             pltpu.VMEM((width, 3 * width), BF16),
@@ -569,7 +591,16 @@
         encoder_proj, norm_gain[None], offset_bias, processor_proj, output_proj, cotangent,
     )
 
-    return (processed[None], gradient)
+    return pl.pallas_call(
+        place_kernel,
+        out_shape=(
+            jax.ShapeDtypeStruct((1, rows, width), BF16),
+            jax.ShapeDtypeStruct((16, width), F32),
+        ),
+        in_specs=[vmem(), vmem()],
+        out_specs=(vmem(), vmem()),
+        name="place",
+    )(processed, gradient)
 
 
 def solution(mesh):

time: 105 us -> 98.9 us (0.942); the launches traced: 105 us -> 97.2 us
  Pallas kernels: 101 us -> 96.6 us
  local copies, waits for them, and re-layouts: 3.34 us -> 0 us
    pallas_call x1, Pallas kernels: 101 us -> 94.7 us  [shards(): pl.pallas_call(layer_kernel, out_shape=(jax.ShapeDtypeStruct((rows, width...]
    unnamed x2 -> x0, local copies, waits for them, and re-layouts: 3.34 us -> none
    pallas_call x0 -> x1, Pallas kernels: none -> 1.88 us  [shards(): pl.pallas_call(place_kernel, out_shape=(jax.ShapeDtypeStruct((1, rows, wi...]
where the time goes in v5:
time: 98.9 us; the launch traced here: 97.2 us
  Pallas kernels  96.6 us (98%)
    pallas_call x1, Pallas kernels, shards(): pl.pallas_call(layer_kernel, out_shape=(jax.ShapeDtypeStruct((rows, width...  94.7 us

profile of v5, /device:TPU:32, one launch (start us, length us, event | category | flops | bytes accessed | tf_op | source)
XLA Modules:
  0.0 97.2 jit_solution(7641467583923782302)
XLA Ops:
  0.6 94.7 %layer.1 = (bf16[256,1024]{1,0:T(8,128)(2,1)}, f32[16,1024]{1,0:T(8,128)}) custom-call(s32[64,128]{1,0:T(8,128)} %bitcast.4, s32[16]{0:T(128)} %windows_ref.1, bf16[1,100,4096]{2,1,0:T(8,128)(2,1)} %grid_ref.1, s32[64,128]{1,0:T(8,128)} %bitcast.5, s32[64,64]{1,0:T(8,128)} %count_ref.1, f32[64,128]{1,0:T(8,128)} %bitcast.6, bf16[256,1024]{1,0:T(8,128)(2,1)} %latent_ref.1, ...), custom_call_target="tpu_custom_call" | custom-call | tf_op jit(solution)/shard_map/layer/pallas_call | solution.py:529
  95.3 1.9 %place.1 = (bf16[1,256,1024]{2,1,0:T(8,128)(2,1)}, f32[16,1024]{1,0:T(8,128)}) custom-call(bf16[256,1024]{1,0:T(8,128)(2,1)} %get-tuple-element.4.processed_ref, f32[16,1024]{1,0:T(8,128)} %get-tuple-element.5.gradient_ref), custom_call_target="tpu_custom_call" | custom-call | tf_op jit(solution)/shard_map/place/pallas_call | solution.py:594

commit v6 on v5

--- a/solution.py
+++ b/solution.py
@@ -28,7 +28,8 @@
     targets, biases, acc, peak_ref, total_ref, send, recv, rest_send, rest_recv,
     big, out_proj, cotangent, fetched, hidden_ref, extended, mixed_rows, offsets, tables,
     attended_t, attended, halo_send, halo_recv, grads, from_core, merged, v_in, v_sum, w_in,
-    r_all, core_send, core_recv, y_send, y_recv, w_send, w_recv, r_send, r_recv,
+    r_all, x_in, x_sum, z_in, y_all, core_send, core_recv, y_send, y_recv, w_send, w_recv,
+    r_send, r_recv, x_send, x_recv, z_send, z_recv, s_send, s_recv,
 ):
     seq = lax.axis_index("seq")
     y = lax.axis_index("dp")
@@ -353,10 +354,11 @@
         )
 
     part_width = width // X
-    strip_width = width // Y
+    half_width = width // 2
+    strip_width = half_width // Y
 
     def strip(who):
-        return pl.ds(pl.multiple_of(who * strip_width, strip_width), strip_width)
+        return pl.ds(pl.multiple_of(half_width + who * strip_width, strip_width), strip_width)
 
     def part_of(turn):
         return (x + 1 + turn) % X
@@ -373,6 +375,13 @@
         return remote(
             merged.at[part, :, :, strip((y + k) % Y)], v_in.at[k - 1, part],
             y_send.at[k - 1, part], y_recv.at[k - 1, part], y_peers[k - 1],
+        )
+
+    def x_copy(turn):
+        part = part_of(turn)
+        return remote(
+            merged.at[part, :, :, pl.ds(0, half_width)], x_in.at[turn], x_send.at[turn],
+            x_recv.at[turn], place(y, part, z, core),
         )
 
     def w_copy(turn, k):
@@ -383,12 +392,14 @@
             place(y, part, to_z, core),
         )
 
-    def pass_to_y(turn):
+    def pass_to_y(turn, with_x):
         part = part_of(turn)
         core_copy(turn).wait_recv()
         merged[part] = (
             grads[part, :, core].astype(F32) + from_core[part].astype(F32)
         ).astype(BF16)
+        if with_x:
+            x_copy(turn).start()
         for k in range(1, Y):
             y_copy(turn, k).start()
 
@@ -415,7 +426,7 @@
         pairs_in_part = part_width // (2 * size)
         for block in range(2):
             if block == 1:
-                pl.when(turn > 0)(lambda: pass_to_y(turn - 1))
+                pl.when(turn > 0)(lambda: pass_to_y(turn - 1, True))
             mine = slice((block + 1) * reach, (block + 2) * reach)
             theirs = slice(block * reach, block * reach + span)
             for pair in range(pairs_in_part):
@@ -460,23 +471,49 @@
             + jnp.dot(attended[...], out_proj[:, at], preferred_element_type=F32)
         ).astype(BF16)
 
-    pass_to_y(X - 1)
-    for turn in range(1, X - 1):
-        pass_to_owners(turn, 0)
-        out_tile(turn - 1)
+    pass_to_y(X - 1, False)
+    pass_to_owners(1, 0)
+    out_tile(0)
+    part = merged[x, :, :, 0:half_width].astype(F32)
+    for turn in range(X - 1):
+        x_copy(turn).wait_recv()
+        part = part + x_in[turn].astype(F32)
+    x_sum[...] = part.astype(BF16)
+    z_copies = [
+        remote(
+            x_sum.at[(z + k) % Z], z_in.at[k - 1], z_send.at[k - 1], z_recv.at[k - 1],
+            place(y, x, (z + k) % Z, core),
+        )
+        for k in range(1, Z)
+    ]
+    for copy in z_copies:
+        copy.start()
+    pass_to_owners(2, 0)
+    out_tile(1)
     pass_to_owners(X - 1, 1)
+
+    def to_dp(ref, send_sem, recv_sem):
+        copies = [
+            remote(ref.at[y], ref.at[y], send_sem.at[k - 1], recv_sem.at[k - 1], y_peers[k - 1])
+            for k in range(1, Y)
+        ]
+        for copy in copies:
+            copy.start()
+        return copies
+
+    total = x_sum[z].astype(F32)
+    for k in range(1, Z):
+        z_copies[k - 1].wait_recv()
+        total = total + z_in[k - 1].astype(F32)
+    y_all[y] = total
+    s_copies = to_dp(y_all, s_send, s_recv)
     total = v_sum[x, z].astype(F32)
     for turn in range(X):
         for k in range(1 if turn == X - 1 else 0, Z):
             w_copy(turn, k).wait_recv()
             total = total + w_in[turn, k].astype(F32)
     r_all[y] = total
-    r_copies = [
-        remote(r_all.at[y], r_all.at[y], r_send.at[k - 1], r_recv.at[k - 1], y_peers[k - 1])
-        for k in range(1, Y)
-    ]
-    for copy in r_copies:
-        copy.start()
+    r_copies = to_dp(r_all, r_send, r_recv)
 
     def sent_step(step, carry):
         to, copy, rest_copy = block_copy(step)
@@ -497,11 +534,17 @@
             y_copy(turn, k).wait_send()
         for k in range(1 if turn == X - 1 else 0, Z):
             w_copy(turn, k).wait_send()
+    for turn in range(X - 1):
+        x_copy(turn).wait_send()
+    for copy in s_copies:
+        copy.wait_recv()
+    gradient_ref[:, 0:half_width] = (y_all[0] + y_all[1]) + (y_all[2] + y_all[3])
     for copy in r_copies:
         copy.wait_recv()
     for k in range(Y):
-        gradient_ref[:, k * strip_width : (k + 1) * strip_width] = r_all[k]
-    for copy in r_copies:
+        at = half_width + k * strip_width
+        gradient_ref[:, at : at + strip_width] = r_all[k]
+    for copy in z_copies + s_copies + r_copies:
         copy.wait_send()
 
 
@@ -523,7 +566,7 @@
     capacity = edge_source.shape[2]
     main = channels // 16 * 16
     chips = shard_count // CORES
-    strip_width = width // Y
+    strip_width = width // 2 // Y
     dma = pltpu.SemaphoreType.DMA
     hbm = pl.BlockSpec(memory_space=pltpu.HBM)
     processed, gradient = pl.pallas_call(
@@ -573,12 +616,22 @@
             pltpu.VMEM((X, Z, 16, strip_width), BF16),
             pltpu.VMEM((X, Z, 16, strip_width), BF16),
             pltpu.VMEM((Y, 16, strip_width), F32),
+            pltpu.VMEM((X - 1, Z, 16, width // 2), BF16),
+            pltpu.VMEM((Z, 16, width // 2), BF16),
+            pltpu.VMEM((Z - 1, 16, width // 2), BF16),
+            pltpu.VMEM((Y, 16, width // 2), F32),
             dma((X,)),
             dma((X,)),
             dma((Y - 1, X)),
             dma((Y - 1, X)),
             dma((X, Z)),
             dma((X, Z)),
+            dma((Y - 1,)),
+            dma((Y - 1,)),
+            dma((X - 1,)),
+            dma((X - 1,)),
+            dma((Z - 1,)),
+            dma((Z - 1,)),
             dma((Y - 1,)),
             dma((Y - 1,)),
         ],

time: 98.9 us -> 97.4 us (0.985); the launches traced: 97.2 us -> 97.2 us
  no operation moved by 1% of the time
where the time goes in v6:
time: 97.4 us; the launch traced here: 97.2 us
  Pallas kernels  96.5 us (99%)
    pallas_call x1, Pallas kernels, shards(): pl.pallas_call(layer_kernel, out_shape=(jax.ShapeDtypeStruct((rows, width...  94.7 us

profile of v6, /device:TPU:32, one launch (start us, length us, event | category | flops | bytes accessed | tf_op | source)
XLA Modules:
  0.0 97.2 jit_solution(3479783659337993426)
XLA Ops:
  0.6 94.7 %layer.1 = (bf16[256,1024]{1,0:T(8,128)(2,1)}, f32[16,1024]{1,0:T(8,128)}) custom-call(s32[64,128]{1,0:T(8,128)} %bitcast.4, s32[16]{0:T(128)} %windows_ref.1, bf16[1,100,4096]{2,1,0:T(8,128)(2,1)} %grid_ref.1, s32[64,128]{1,0:T(8,128)} %bitcast.5, s32[64,64]{1,0:T(8,128)} %count_ref.1, f32[64,128]{1,0:T(8,128)} %bitcast.6, bf16[256,1024]{1,0:T(8,128)(2,1)} %latent_ref.1, ...), custom_call_target="tpu_custom_call" | custom-call | tf_op jit(solution)/shard_map/layer/pallas_call | solution.py:572
  95.3 1.9 %place.1 = (bf16[1,256,1024]{2,1,0:T(8,128)(2,1)}, f32[16,1024]{1,0:T(8,128)}) custom-call(bf16[256,1024]{1,0:T(8,128)(2,1)} %get-tuple-element.4.processed_ref, f32[16,1024]{1,0:T(8,128)} %get-tuple-element.5.gradient_ref), custom_call_target="tpu_custom_call" | custom-call | tf_op jit(solution)/shard_map/place/pallas_call | solution.py:647
